TPU v7x, 128 devices: a whole 4x4x4 slice. The times are simulated.
128 devices in a mesh: seq: 32 (over z, y, core), head: 4 (over x).
Axes of the slice: x: 4, y: 4, z: 4, core: 2. Of those that a mesh axis runs over, the one named last changes fastest.
Arguments:
- queries: bfloat16 [32768, 8, 128], P('seq', 'head'), may hold values from -6 to 6
- key_rows: bfloat16 [32768, 8, 128], P('seq', 'head'), may hold values from -6 to 6
- value_rows: bfloat16 [32768, 8, 128], P('seq', 'head'), may hold values from -6 to 6
- level_weights: float32 [16, 8, 32768], P(None, 'head', 'seq'), may hold values from 0.25 to 2
- out_weight: bfloat16 [8, 128, 2048], P('head'), may hold values from -0.1875 to 0.1875
- out_grad: bfloat16 [32768, 2048], P('seq', 'head'), may hold values from -6 to 6
Outputs:
- layer_out: bfloat16 [32768, 2048], P('seq', 'head')
- query_grad: bfloat16 [32768, 8, 128], P('seq', 'head')
- key_grad: bfloat16 [32768, 8, 128], P('seq', 'head')
- value_grad: bfloat16 [32768, 8, 128], P('seq', 'head')
- weight_grad: float32 [16, 8, 32768], P(None, 'head', 'seq')
All inputs are finite; a program needn't handle non-finite values.
Results may differ from a plain program's by a relative error of at most 0.017.
Values may be sent and summed in bfloat16 or wider, within the bound.
A program may use at most 192 MiB of HBM per device.

v0:
```python
import functools

import jax
import jax.numpy as jnp
from jax import lax
from jax.experimental import pallas as pl
from jax.experimental.pallas import tpu as pltpu
from jax.sharding import PartitionSpec as P

MESH = pl.DeviceIdType.MESH
F32 = jnp.float32
BF16 = jnp.bfloat16
LEVEL_GAIN = 0.02
BLK = 128
DIAG_LEVELS = 8
LOCAL_LEVELS = 11


def scale_of(level):
    return LEVEL_GAIN * 2.0 ** (-0.5 * max(level - 1, 0))


LOCAL_PAIRS = [(0, 1, 1), (0, 3, 1), (0, 5, 1), (0, 7, 1), (1, 2, 2), (1, 6, 2), (2, 4, 4)]


def mm(a, b):
    return jnp.dot(a, b, preferred_element_type=F32)


def mm_nt(a, b):
    return lax.dot_general(a, b, (((1,), (1,)), ((), ())), preferred_element_type=F32)


def kernel(
    dev_bits, q_ref, k_ref, v_ref, lw_ref, w_hbm, og_ref,
    lo_ref, dq_ref, dk_ref, dv_ref, wg_ref,
    wall, wsc, lev_ref, qt, kt, vt, gt, wq, st_ref, mix_ref, near, tb, tl, tlt, ot,
    sb, rb, cb, rcb, tst, tstt, lg, xf, llg,
    p2, alone, pf, summed, r1, rdir, hall, dqa, dka, dva, acc,
    own_sem, w_send, w_recv, f_send, f_recv, b_send, b_recv, c_send, c_recv, r_send, r_recv, h_send, h_recv,
):
    me_s = lax.axis_index("seq")
    me_h = lax.axis_index("head")
    core = lax.rem(me_s, 2)
    right, left, across = lax.rem(me_h + 1, 4), lax.rem(me_h + 3, 4), lax.rem(me_h + 2, 4)

    def partner(step):
        bit = 1 << step
        has = lax.rem(lax.div(me_s, bit), 2)
        return me_s + bit - 2 * bit * has, has

    def send(src, dst, send_sem, recv_sem, seq, head):
        copy = pltpu.make_async_remote_copy(
            src_ref=src, dst_ref=dst, send_sem=send_sem, recv_sem=recv_sem,
            device_id=(seq, head), device_id_type=MESH,
        )
        copy.start()
        return copy

    barrier = pltpu.get_barrier_semaphore()
    for other in (right, left, across):
        pl.semaphore_signal(barrier, inc=1, device_id=(me_s, other), device_id_type=MESH)
    for step in range(dev_bits):
        pl.semaphore_signal(barrier, inc=1, device_id=(partner(step)[0], me_h), device_id_type=MESH)
    pl.semaphore_wait(barrier, 3 + dev_bits)

    own = pltpu.make_async_copy(w_hbm.at[:, pl.ds(pl.multiple_of(me_h * 512, 512), 512)], wall.at[0], own_sem)
    half = pl.ds(pl.multiple_of(core * 128, 128), 128)
    w_copies = {}
    for k in (2, 1, 3):
        to = lax.rem(me_h + k, 4)
        w_copies[k] = send(
            w_hbm.at[half, pl.ds(pl.multiple_of(to * 512, 512), 512)], wall.at[k, half],
            w_send.at[k - 1], w_recv.at[k - 1], me_s, to)
    own.start()
    sibling = partner(0)[0]
    f_copies = {}

    def forward_weights(k):
        w_copies[k].wait_recv()
        f_copies[k] = send(wall.at[k, half], wall.at[k, half], f_send.at[k - 1], f_recv.at[k - 1], sibling, me_h)

    row_id = lax.broadcasted_iota(jnp.int32, (BLK, BLK), 0)
    col_id = lax.broadcasted_iota(jnp.int32, (BLK, BLK), 1)
    apart = row_id ^ col_id
    level = jnp.zeros((BLK, BLK), jnp.int32)
    for bit in range(7):
        level = level + ((apart >> bit) > 0).astype(jnp.int32)
    lev_ref[...] = jnp.where(row_id <= col_id, level, -1)

    def cols_of(b):
        return pl.ds(pl.multiple_of(b * BLK, BLK), BLK)

    @pl.loop(0, 8)
    def _(b):
        cols = cols_of(b)
        for h in range(2):
            lanes = slice(h * 128, h * 128 + 128)
            kb, vb = k_ref[cols, lanes].T, v_ref[cols, lanes].T
            kt[h, :, cols] = kb
            vt[h, :, cols] = vb
            tb[h, b] = mm_nt(kb, vb)

    total = []
    for h in range(2):
        t = [tb[h, b] for b in range(8)]
        pairs = [t[2 * i] + t[2 * i + 1] for i in range(4)]
        quads = [pairs[0] + pairs[1], pairs[2] + pairs[3]]
        for slot, value in enumerate([t[0], t[2], t[4], t[6], pairs[0], pairs[2], quads[0]]):
            tl[h, slot] = value.astype(BF16)
            tlt[h, slot] = value.T.astype(BF16)
        xf[h] = quads[0] + quads[1]

    b_copies = []

    def send_states(step):
        for h in range(2):
            sb[step, h] = xf[h].astype(BF16)
        b_copies.append(send(sb.at[step], rb.at[step], b_send.at[step], b_recv.at[step], partner(step)[0], me_h))

    def take_states(step):
        b_copies[step].wait_recv()
        has = partner(step)[1].astype(F32)
        for h in range(2):
            got = rb[step, h].astype(F32)
            xf[h] = xf[h] + got
            kept = got * has
            tst[h, step] = kept.astype(BF16)
            tstt[h, :, step * 128:step * 128 + 128] = kept.T.astype(BF16)

    send_states(0)
    forward_weights(2)

    for h in range(2):
        for l in range(LOCAL_LEVELS + dev_bits):
            wsc[h, l:l + 1, :] = lw_ref[l, h:h + 1, :] * scale_of(l)

    @pl.loop(0, 8)
    def _(b):
        cols = cols_of(b)
        for h in range(2):
            qb = q_ref[cols, h * 128:h * 128 + 128].T
            qt[h, :, cols] = qb
            qf = qb.astype(F32)
            for c in range(3 + dev_bits):
                wq[h, c, :, cols] = (qf * wsc[h, DIAG_LEVELS + c:DIAG_LEVELS + c + 1, cols]).astype(BF16)

    right_msgs, left_msgs = {}, {}

    def send_right(i, src, dst):
        right_msgs[i] = send(src, dst, r_send.at[i], r_recv.at[i], me_s, right)

    def send_left(i, src, dst):
        left_msgs[i] = send(src, dst, r_send.at[6 + i], r_recv.at[6 + i], me_s, left)

    def partial_grad(k, u, j):
        rows = slice(u * 512 + j * 256, u * 512 + j * 256 + 256)
        return mm_nt(wall[k], og_ref[rows, :])

    f_copies[2].wait_recv()
    for u in range(2):
        for j in range(2):
            part = partial_grad(2, u, j).astype(BF16)
            p2[0, u, :, j * 256:j * 256 + 256] = part[:128]
            p2[1, u, :, j * 256:j * 256 + 256] = part[128:]
        send_right(u, p2.at[0, u], r1.at[0, u])
        send_left(u, p2.at[1, u], r1.at[1, u])

    forward_weights(1)
    forward_weights(3)
    take_states(0)
    send_states(1)

    def diag_forward(b):
        cols = cols_of(b)
        for h in range(2):
            lev = lev_ref[...]
            mix = jnp.zeros((BLK, BLK), F32)
            for l in range(DIAG_LEVELS):
                mix = jnp.where(lev == l, wsc[h, l:l + 1, cols], mix)
            scores = mm(k_ref[cols, h * 128:h * 128 + 128], qt[h, :, cols])
            weighted = (mix * scores).astype(BF16)
            st_ref[h, b] = scores
            mix_ref[h, b] = mix
            near[h, b] = weighted
            ot[h, :, cols] = mm(vt[h, :, cols], weighted)

    pl.loop(0, 4)(diag_forward)
    f_copies[1].wait_recv()
    f_copies[3].wait_recv()
    for u in range(2):
        for j in range(2):
            at = slice(j * 256, j * 256 + 256)
            part = partial_grad(3, u, j)
            pf[0, u, :, at] = part[:128]
            alone[0, u, :, at] = part[128:].astype(BF16)
            part = partial_grad(1, u, j)
            alone[1, u, :, at] = part[:128].astype(BF16)
            pf[1, u, :, at] = part[128:]
        send_right(2 + u, alone.at[0, u], rdir.at[0, 1, u])
        send_left(2 + u, alone.at[1, u], rdir.at[1, 0, u])
    take_states(1)
    send_states(2)
    pl.loop(4, 8)(diag_forward)

    for u in range(2):
        right_msgs[u].wait_recv()
        summed[0, u] = (pf[0, u] + r1[0, u].astype(F32)).astype(BF16)
        send_right(4 + u, summed.at[0, u], rdir.at[0, 0, u])
        left_msgs[u].wait_recv()
        summed[1, u] = (pf[1, u] + r1[1, u].astype(F32)).astype(BF16)
        send_left(4 + u, summed.at[1, u], rdir.at[1, 1, u])
    take_states(2)
    if dev_bits > 3:
        send_states(3)

    for h in range(2):
        for slot, (c, first, size) in enumerate(LOCAL_PAIRS):
            at = slice(first * BLK, (first + size) * BLK)
            ot[h, :, at] = ot[h, :, at] + mm(tlt[h, slot], wq[h, c, :, at])

    own.wait()
    for u in range(2):
        for j in range(2):
            at = slice(j * 256, j * 256 + 256)
            part = partial_grad(0, u, j)
            pf[0, u, :, at] = part[:128]
            pf[1, u, :, at] = part[128:]
    for step in range(3, dev_bits):
        take_states(step)
        if step + 1 < dev_bits:
            send_states(step + 1)

    @pl.loop(0, 8)
    def _(b):
        cols = cols_of(b)
        for h in range(2):
            far = mm(tstt[h], wq[h, 3:, :, cols].reshape(dev_bits * 128, BLK))
            hall[0, cols, h * 128:h * 128 + 128] = (ot[h, :, cols] + far).T.astype(BF16)

    h_copies = {}

    def send_heads(i, slot, part, to_slot, head):
        rows = slice(part * 512, part * 512 + 512)
        h_copies[i] = send(hall.at[slot, rows], hall.at[to_slot, rows], h_send.at[i], h_recv.at[i], me_s, head)

    send_heads(0, 0, 0, 1, right)
    send_heads(1, 0, 1, 3, left)
    send_heads(2, 0, 1, 1, right)
    send_heads(3, 0, 0, 3, left)

    for u in range(2):
        at = slice(u * 512, u * 512 + 512)
        right_msgs[2 + u].wait_recv()
        left_msgs[2 + u].wait_recv()
        right_msgs[4 + u].wait_recv()
        left_msgs[4 + u].wait_recv()
        for h in range(2):
            gt[h, :, at] = (pf[h, u] + rdir[0, h, u].astype(F32) + rdir[1, h, u].astype(F32)).astype(BF16)

    for h in range(2):
        grads = mm_nt(wq[h, 3:].reshape(dev_bits * 128, 1024), gt[h])
        for step in range(dev_bits):
            lg[h, step] = grads[step * 128:step * 128 + 128]
        xf[h] = jnp.zeros((128, 128), F32)

    c_copies = {}

    def send_grads(step):
        to, has = partner(step)
        for h in range(2):
            cb[step, h] = (xf[h] + lg[h, step] * has.astype(F32)).astype(BF16)
        c_copies[step] = send(cb.at[step], rcb.at[step], c_send.at[step], c_recv.at[step], to, me_h)

    def take_grads(step):
        c_copies[step].wait_recv()
        for h in range(2):
            xf[h] = xf[h] + rcb[step, h].astype(F32)

    def diag_backward(b):
        cols = cols_of(b)
        for h in range(2):
            lev = lev_ref[...]
            gb = gt[h, :, cols]
            grad_scores = mm(v_ref[cols, h * 128:h * 128 + 128], gb)
            weighted = (mix_ref[h, b] * grad_scores).astype(BF16)
            product = grad_scores * st_ref[h, b]
            dqa[h, :, cols] = mm(kt[h, :, cols], weighted)
            dka[h, :, cols] = mm_nt(qt[h, :, cols], weighted)
            dva[h, :, cols] = mm_nt(gb, near[h, b])
            for l in range(DIAG_LEVELS):
                summed_l = jnp.sum(jnp.where(lev == l, product, 0.0), axis=0, keepdims=True)
                wg_ref[l, h:h + 1, cols] = summed_l * scale_of(l)

    def far_backward(b):
        cols = cols_of(b)
        for h in range(2):
            gb = gt[h, :, cols]
            qf = qt[h, :, cols].astype(F32)
            sums = dqa[h, :, cols]
            for step in range(dev_bits):
                l = LOCAL_LEVELS + step
                got = mm(tst[h, step], gb)
                sums = sums + got * wsc[h, l:l + 1, cols]
                wg_ref[l, h:h + 1, cols] = jnp.sum(got * qf, axis=0, keepdims=True) * scale_of(l)
            dqa[h, :, cols] = sums

    def local_backward(h):
        for l in range(DIAG_LEVELS, LOCAL_LEVELS):
            wg_ref[l, h:h + 1, :] = jnp.zeros((1, 1024), F32)
        for slot, (c, first, size) in enumerate(LOCAL_PAIRS):
            at = slice(first * BLK, (first + size) * BLK)
            l = DIAG_LEVELS + c
            gb = gt[h, :, at]
            got = mm(tl[h, slot], gb)
            dqa[h, :, at] = dqa[h, :, at] + got * wsc[h, l:l + 1, at]
            wg_ref[l, h:h + 1, at] = jnp.sum(got * qt[h, :, at].astype(F32), axis=0, keepdims=True) * scale_of(l)
            llg[h, slot] = mm_nt(wq[h, c, :, at], gb)

    work = [
        lambda: pl.loop(0, 4)(diag_backward),
        lambda: pl.loop(4, 8)(diag_backward),
        lambda: pl.loop(0, 4)(far_backward),
        lambda: pl.loop(4, 8)(far_backward),
        lambda: [local_backward(h) for h in range(2)],
    ]
    relayed = 0
    for step in reversed(range(dev_bits)):
        send_grads(step)
        if work:
            work.pop(0)()
        take_grads(step)
        if step == dev_bits - 2:
            h_copies[0].wait_recv()
            send_heads(4, 1, 0, 2, right)
            h_copies[1].wait_recv()
            send_heads(5, 3, 1, 2, left)
    for item in work:
        item()

    @pl.loop(0, 8)
    def _(b):
        cols = cols_of(b)
        for h in range(2):
            dq_ref[cols, h * 128:h * 128 + 128] = dqa[h, :, cols].T.astype(BF16)

    for b in range(8):
        at = slice(b * BLK, b * BLK + BLK)
        for h in range(2):
            x = xf[h]
            for slot, (c, first, size) in enumerate(LOCAL_PAIRS):
                if first - size <= b < first:
                    x = x + llg[h, slot]
            dk = dka[h, :, at] + mm(x.astype(BF16), vt[h, :, at])
            dv = dva[h, :, at] + mm(x.T.astype(BF16), kt[h, :, at])
            dk_ref[at, h * 128:h * 128 + 128] = dk.T.astype(BF16)
            dv_ref[at, h * 128:h * 128 + 128] = dv.T.astype(BF16)

    @pl.loop(0, 4)
    def _(b):
        rows = pl.ds(pl.multiple_of(b * 256, 256), 256)
        acc[rows, :] = mm(hall[0, rows, :], wall[0])

    h_copies[2].wait_recv()
    h_copies[3].wait_recv()

    @pl.loop(0, 4)
    def _(b):
        rows = pl.ds(pl.multiple_of(b * 256, 256), 256)
        acc[rows, :] = acc[rows, :] + mm(hall[1, rows, :], wall[1]) + mm(hall[3, rows, :], wall[3])

    h_copies[4].wait_recv()
    h_copies[5].wait_recv()

    @pl.loop(0, 4)
    def _(b):
        rows = pl.ds(pl.multiple_of(b * 256, 256), 256)
        lo_ref[rows, :] = (acc[rows, :] + mm(hall[2, rows, :], wall[2])).astype(BF16)

    for group in (w_copies, f_copies, right_msgs, left_msgs, h_copies, c_copies):
        for copy in group.values():
            copy.wait_send()
    for copy in b_copies:
        copy.wait_send()


def per_device(queries, key_rows, value_rows, level_weights, out_weight, out_grad):
    dev_bits = lax.axis_size("seq").bit_length() - 1
    dma = pltpu.SemaphoreType.DMA
    vmem = pltpu.VMEM
    full = pl.BlockSpec(memory_space=pltpu.VMEM)
    stack = 3 + dev_bits
    outs = pl.pallas_call(
        functools.partial(kernel, dev_bits),
        out_shape=(
            jax.ShapeDtypeStruct((1024, 512), BF16),
            jax.ShapeDtypeStruct((1024, 256), BF16),
            jax.ShapeDtypeStruct((1024, 256), BF16),
            jax.ShapeDtypeStruct((1024, 256), BF16),
            jax.ShapeDtypeStruct(level_weights.shape, F32),
        ),
        in_specs=[full, full, full, full, pl.BlockSpec(memory_space=pl.ANY), full],
        out_specs=[full] * 5,
        scratch_shapes=[
            vmem((4, 256, 512), BF16),
            vmem((2, LOCAL_LEVELS + dev_bits, 1024), F32),
            vmem((BLK, BLK), jnp.int32),
            vmem((2, 128, 1024), BF16),
            vmem((2, 128, 1024), BF16),
            vmem((2, 128, 1024), BF16),
            vmem((2, 128, 1024), BF16),
            vmem((2, stack, 128, 1024), BF16),
            vmem((2, 8, BLK, BLK), F32),
            vmem((2, 8, BLK, BLK), F32),
            vmem((2, 8, BLK, BLK), BF16),
            vmem((2, 8, 128, 128), F32),
            vmem((2, 7, 128, 128), BF16),
            vmem((2, 7, 128, 128), BF16),
            vmem((2, 128, 1024), F32),
            vmem((dev_bits, 2, 128, 128), BF16),
            vmem((dev_bits, 2, 128, 128), BF16),
            vmem((dev_bits, 2, 128, 128), BF16),
            vmem((dev_bits, 2, 128, 128), BF16),
            vmem((2, dev_bits, 128, 128), BF16),
            vmem((2, 128, dev_bits * 128), BF16),
            vmem((2, dev_bits, 128, 128), F32),
            vmem((2, 128, 128), F32),
            vmem((2, 7, 128, 128), F32),
            vmem((2, 2, 128, 512), BF16),
            vmem((2, 2, 128, 512), BF16),
            vmem((2, 2, 128, 512), F32),
            vmem((2, 2, 128, 512), BF16),
            vmem((2, 2, 128, 512), BF16),
            vmem((2, 2, 2, 128, 512), BF16),
            vmem((4, 1024, 256), BF16),
            vmem((2, 128, 1024), F32),
            vmem((2, 128, 1024), F32),
            vmem((2, 128, 1024), F32),
            vmem((1024, 512), F32),
            dma,
            dma((3,)), dma((3,)), dma((3,)), dma((3,)),
            dma((dev_bits,)), dma((dev_bits,)), dma((dev_bits,)), dma((dev_bits,)),
            dma((12,)), dma((12,)), dma((6,)), dma((6,)),
        ],
        compiler_params=pltpu.CompilerParams(
            collective_id=0, has_side_effects=True, vmem_limit_bytes=56 * 1024 * 1024),
        cost_estimate=pl.CostEstimate(flops=6 * 10**9, bytes_accessed=8 * 2**20, transcendentals=0),
    )(
        queries.reshape(1024, 256), key_rows.reshape(1024, 256), value_rows.reshape(1024, 256),
        level_weights, out_weight.reshape(256, 2048), out_grad,
    )
    layer_out, dq, dk, dv, wg = outs
    shape = queries.shape
    return layer_out, dq.reshape(shape), dk.reshape(shape), dv.reshape(shape), wg


def solution(mesh):
    in_specs = (
        P("seq", "head", None),
        P("seq", "head", None),
        P("seq", "head", None),
        P(None, "head", "seq"),
        P("head", None, None),
        P("seq", "head"),
    )
    out_specs = (
        P("seq", "head"),
        P("seq", "head", None),
        P("seq", "head", None),
        P("seq", "head", None),
        P(None, "head", "seq"),
    )
    return jax.shard_map(
        per_device, mesh=mesh, in_specs=in_specs, out_specs=out_specs, check_vma=False
    )
```

profile of v0, /device:TPU:1, one launch (start us, length us, event | category | flops | bytes accessed | tf_op | source)
XLA Modules:
  0.0 71.6 jit_solution(16639370431885406424)
XLA Ops:
  0.6 0.0 copy-start.3
  0.6 0.0 copy-start.4
  0.7 2.0 %copy.17 = bf16[128,8,2,128]{3,1,2,0:T(8,128)(2,1)} copy(bf16[128,8,2,128]{3,2,1,0:T(2,128)(2,1)} %bitcast.11) | data formatting | bytes 1048576
  2.7 0.0 copy-done.3
  2.7 0.0 copy-done.4
  2.7 1.1 %copy_bitcast_fusion = (bf16[1024,256]{1,0:T(8,128)(2,1)}, bf16[1024,256]{1,0:T(8,128)(2,1)}) fusion(bf16[128,8,2,128]{3,2,1,0:T(2,128)(2,1)S(1)} %bitcast.13, bf16[128,8,2,128]{3,2,1,0:T(2,128)(2,1)S(1)} %bitcast.14), kind=kLoop, calls=%fused_computation | loop fusion | bytes 2097152 | tf_op jit(solution)/shard_map/reshape | solution.py:449
  3.8 62.3 %shard_map.101 = (bf16[1024,512]{1,0:T(8,128)(2,1)}, bf16[1024,256]{1,0:T(8,128)(2,1)}, bf16[1024,256]{1,0:T(8,128)(2,1)}, bf16[1024,256]{1,0:T(8,128)(2,1)}, f32[16,2,1024]{2,1,0:T(2,128)}) custom-call(bf16[1024,256]{1,0:T(8,128)(2,1)} %bitcast.12, bf16[1024,256]{1,0:T(8,128)(2,1)} %get-tuple-element.16.k_ref, bf16[1024,256]{1,0:T(8,128)(2,1)} %get-tuple-element.15.v_ref, ...), custom_call_target="tpu_custom_call" | custom-call | flops 6000000000 | bytes 8388608 | tf_op jit(solution)/shard_map/pallas_call | solution.py:393
  66.0 0.0 copy-start.2
  66.1 0.0 copy-start.1
  66.1 2.0 %reshape.35 = bf16[1024,2,128]{2,1,0:T(2,128)(2,1)} reshape(bf16[1024,256]{1,0:T(8,128)(2,1)} %get-tuple-element.11) | data formatting | bytes 1048576 | tf_op jit(solution)/shard_map/reshape | solution.py:454
  68.1 0.0 copy-done.2
  68.1 0.0 copy-start
  68.1 0.9 %reshape.36 = bf16[1024,2,128]{2,1,0:T(2,128)(2,1)} reshape(bf16[1024,256]{1,0:T(8,128)(2,1)S(1)} %copy-done.2) | data formatting | bytes 1048576 | tf_op jit(solution)/shard_map/reshape | solution.py:454
  69.0 0.0 copy-done.1
  69.0 0.9 %reshape.37 = bf16[1024,2,128]{2,1,0:T(2,128)(2,1)} reshape(bf16[1024,256]{1,0:T(8,128)(2,1)S(1)} %copy-done.1) | data formatting | bytes 1048576 | tf_op jit(solution)/shard_map/reshape | solution.py:454
  70.0 0.0 copy-done
  70.0 0.0 copy-start.5
  70.0 1.0 %copy.20 = bf16[1024,512]{1,0:T(8,128)(2,1)} copy(bf16[1024,512]{1,0:T(8,128)(2,1)S(1)} %copy-done) | data formatting | bytes 2097152
  70.9 0.1 copy-done.5
  71.0 0.7 copy.21
Async XLA Ops:
  0.6 2.0 %copy-start.3 = (bf16[1024,2,128]{2,1,0:T(2,128)(2,1)S(1)}, bf16[1024,2,128]{2,1,0:T(2,128)(2,1)}, u32[]{:S(2)}) copy-start(bf16[1024,2,128]{2,1,0:T(2,128)(2,1)} %param.8) | copy-start | bytes 1572868
  0.6 2.0 %copy-start.4 = (bf16[1024,2,128]{2,1,0:T(2,128)(2,1)S(1)}, bf16[1024,2,128]{2,1,0:T(2,128)(2,1)}, u32[]{:S(2)}) copy-start(bf16[1024,2,128]{2,1,0:T(2,128)(2,1)} %param.7) | copy-start | bytes 1572868
  66.0 2.1 %copy-start.2 = (bf16[1024,256]{1,0:T(8,128)(2,1)S(1)}, bf16[1024,256]{1,0:T(8,128)(2,1)}, u32[]{:S(2)}) copy-start(bf16[1024,256]{1,0:T(8,128)(2,1)} %get-tuple-element.12) | copy-start | bytes 1572868
  66.1 3.0 %copy-start.1 = (bf16[1024,256]{1,0:T(8,128)(2,1)S(1)}, bf16[1024,256]{1,0:T(8,128)(2,1)}, u32[]{:S(2)}) copy-start(bf16[1024,256]{1,0:T(8,128)(2,1)} %get-tuple-element.13) | copy-start | bytes 1572868
  68.1 1.8 %copy-start = (bf16[1024,512]{1,0:T(8,128)(2,1)S(1)}, bf16[1024,512]{1,0:T(8,128)(2,1)}, u32[]{:S(2)}) copy-start(bf16[1024,512]{1,0:T(8,128)(2,1)} %get-tuple-element.22) | copy-start | bytes 3145732
  70.0 1.0 %copy-start.5 = (f32[16,2,1024]{2,1,0:T(2,128)S(1)}, f32[16,2,1024]{2,1,0:T(2,128)}, u32[]{:S(2)}) copy-start(f32[16,2,1024]{2,1,0:T(2,128)} %get-tuple-element.26) | copy-start | bytes 393220
where the time goes:
time: 71.8 us; the launch traced here: 71.6 us
  Pallas kernels  62.3 us (87%)
  local copies, waits for them, and re-layouts  8.7 us (12%)
    pallas_call x1, Pallas kernels, per_device(): pl.pallas_call(functools.partial(kernel, dev_bits), out_shape=(jax.ShapeD...  62.3 us
    unnamed x15, local copies, waits for them, and re-layouts  3.7 us
    reshape x1, local copies, waits for them, and re-layouts, per_device(): dq.reshape(shape)  2.04 us

commit v1 on v0

--- a/solution.py
+++ b/solution.py
@@ -13,6 +13,8 @@
 LEVEL_GAIN = 0.02
 BLK = 128
 DIAG_LEVELS = 8
+DEV_BITS = 5
+PHASES = ((0,), (1, 2, 3), (4, 5, 6))
 LOCAL_LEVELS = 11
 
 
@@ -32,22 +34,33 @@
 
 
 def kernel(
-    dev_bits, q_ref, k_ref, v_ref, lw_ref, w_hbm, og_ref,
-    lo_ref, dq_ref, dk_ref, dv_ref, wg_ref,
+    q_in, k_in, v_in, lw_in, w_hbm, og_in,
+    lo_out, dq_out, dk_out, dv_out, wg_out,
+    q_ref, k_ref, v_ref, lw_ref, og_ref, lo_ref, dq_ref, dk_ref, dv_ref, wg_ref, kn, vn,
     wall, wsc, lev_ref, qt, kt, vt, gt, wq, st_ref, mix_ref, near, tb, tl, tlt, ot,
     sb, rb, cb, rcb, tst, tstt, lg, xf, llg,
     p2, alone, pf, summed, r1, rdir, hall, dqa, dka, dva, acc,
-    own_sem, w_send, w_recv, f_send, f_recv, b_send, b_recv, c_send, c_recv, r_send, r_recv, h_send, h_recv,
+    in_sem, out_sem, own_sem, w_send, w_recv, f_send, f_recv, b_send, b_recv, c_send, c_recv, r_send, r_recv, h_send, h_recv,
 ):
     me_s = lax.axis_index("seq")
     me_h = lax.axis_index("head")
     core = lax.rem(me_s, 2)
     right, left, across = lax.rem(me_h + 1, 4), lax.rem(me_h + 3, 4), lax.rem(me_h + 2, 4)
 
+    def bit_of(bit):
+        return lax.rem(lax.div(me_s, 1 << bit), 2)
+
+    def flipped(bits):
+        to = me_s
+        for bit in bits:
+            to = to + (1 << bit) - (2 << bit) * bit_of(bit)
+        return to
+
     def partner(step):
-        bit = 1 << step
-        has = lax.rem(lax.div(me_s, bit), 2)
-        return me_s + bit - 2 * bit * has, has
+        if step == 0:
+            return flipped([0])
+        low, j = (1, step) if step < 4 else (3, step - 3)
+        return flipped([low + i for i in range(2) if j >> i & 1])
 
     def send(src, dst, send_sem, recv_sem, seq, head):
         copy = pltpu.make_async_remote_copy(
@@ -57,12 +70,17 @@
         copy.start()
         return copy
 
+    loads = []
+    for n, (src, dst) in enumerate([(k_in, k_ref), (v_in, v_ref), (lw_in, lw_ref), (q_in, q_ref), (og_in, og_ref)]):
+        loads.append(pltpu.make_async_copy(src, dst, in_sem.at[n]))
+        loads[n].start()
+
     barrier = pltpu.get_barrier_semaphore()
     for other in (right, left, across):
         pl.semaphore_signal(barrier, inc=1, device_id=(me_s, other), device_id_type=MESH)
-    for step in range(dev_bits):
-        pl.semaphore_signal(barrier, inc=1, device_id=(partner(step)[0], me_h), device_id_type=MESH)
-    pl.semaphore_wait(barrier, 3 + dev_bits)
+    for step in range(7):
+        pl.semaphore_signal(barrier, inc=1, device_id=(partner(step), me_h), device_id_type=MESH)
+    pl.semaphore_wait(barrier, 10)
 
     own = pltpu.make_async_copy(w_hbm.at[:, pl.ds(pl.multiple_of(me_h * 512, 512), 512)], wall.at[0], own_sem)
     half = pl.ds(pl.multiple_of(core * 128, 128), 128)
@@ -73,7 +91,7 @@
             w_hbm.at[half, pl.ds(pl.multiple_of(to * 512, 512), 512)], wall.at[k, half],
             w_send.at[k - 1], w_recv.at[k - 1], me_s, to)
     own.start()
-    sibling = partner(0)[0]
+    sibling = partner(0)
     f_copies = {}
 
     def forward_weights(k):
@@ -91,12 +109,18 @@
     def cols_of(b):
         return pl.ds(pl.multiple_of(b * BLK, BLK), BLK)
 
+    loads[0].wait()
+    loads[1].wait()
+
     @pl.loop(0, 8)
     def _(b):
         cols = cols_of(b)
+        k_all, v_all = k_ref[cols].reshape(BLK, 256), v_ref[cols].reshape(BLK, 256)
         for h in range(2):
             lanes = slice(h * 128, h * 128 + 128)
-            kb, vb = k_ref[cols, lanes].T, v_ref[cols, lanes].T
+            kn[h, cols, :] = k_all[:, lanes]
+            vn[h, cols, :] = v_all[:, lanes]
+            kb, vb = k_all[:, lanes].T, v_all[:, lanes].T
             kt[h, :, cols] = kb
             vt[h, :, cols] = vb
             tb[h, b] = mm_nt(kb, vb)
@@ -111,38 +135,51 @@
             tlt[h, slot] = value.T.astype(BF16)
         xf[h] = quads[0] + quads[1]
 
-    b_copies = []
-
-    def send_states(step):
-        for h in range(2):
-            sb[step, h] = xf[h].astype(BF16)
-        b_copies.append(send(sb.at[step], rb.at[step], b_send.at[step], b_recv.at[step], partner(step)[0], me_h))
-
-    def take_states(step):
-        b_copies[step].wait_recv()
-        has = partner(step)[1].astype(F32)
-        for h in range(2):
-            got = rb[step, h].astype(F32)
-            xf[h] = xf[h] + got
-            kept = got * has
-            tst[h, step] = kept.astype(BF16)
-            tstt[h, :, step * 128:step * 128 + 128] = kept.T.astype(BF16)
+    b_copies = {}
+
+    def send_states(phase):
+        for h in range(2):
+            sb[phase, h] = xf[h].astype(BF16)
+        for step in PHASES[phase]:
+            b_copies[step] = send(sb.at[phase], rb.at[step], b_send.at[step], b_recv.at[step], partner(step), me_h)
+
+    def keep_state(h, slot, value):
+        kept = value * bit_of(slot).astype(F32)
+        tst[h, slot * 128:slot * 128 + 128, :] = kept.astype(BF16)
+        tstt[h, :, slot * 128:slot * 128 + 128] = kept.T.astype(BF16)
+
+    def take_states(phase):
+        for step in PHASES[phase]:
+            b_copies[step].wait_recv()
+        for h in range(2):
+            got = [rb[step, h].astype(F32) for step in PHASES[phase]]
+            if phase == 0:
+                keep_state(h, 0, got[0])
+                xf[h] = xf[h] + got[0]
+            else:
+                far = got[1] + got[2]
+                keep_state(h, 2 * phase - 1, got[0])
+                keep_state(h, 2 * phase, far)
+                xf[h] = xf[h] + got[0] + far
 
     send_states(0)
     forward_weights(2)
+    loads[2].wait()
+    loads[3].wait()
 
     for h in range(2):
-        for l in range(LOCAL_LEVELS + dev_bits):
+        for l in range(LOCAL_LEVELS + DEV_BITS):
             wsc[h, l:l + 1, :] = lw_ref[l, h:h + 1, :] * scale_of(l)
 
     @pl.loop(0, 8)
     def _(b):
         cols = cols_of(b)
-        for h in range(2):
-            qb = q_ref[cols, h * 128:h * 128 + 128].T
+        q_all = q_ref[cols].reshape(BLK, 256)
+        for h in range(2):
+            qb = q_all[:, h * 128:h * 128 + 128].T
             qt[h, :, cols] = qb
             qf = qb.astype(F32)
-            for c in range(3 + dev_bits):
+            for c in range(3 + DEV_BITS):
                 wq[h, c, :, cols] = (qf * wsc[h, DIAG_LEVELS + c:DIAG_LEVELS + c + 1, cols]).astype(BF16)
 
     right_msgs, left_msgs = {}, {}
@@ -157,6 +194,9 @@
         rows = slice(u * 512 + j * 256, u * 512 + j * 256 + 256)
         return mm_nt(wall[k], og_ref[rows, :])
 
+    take_states(0)
+    send_states(1)
+    loads[4].wait()
     f_copies[2].wait_recv()
     for u in range(2):
         for j in range(2):
@@ -168,8 +208,6 @@
 
     forward_weights(1)
     forward_weights(3)
-    take_states(0)
-    send_states(1)
 
     def diag_forward(b):
         cols = cols_of(b)
@@ -178,7 +216,7 @@
             mix = jnp.zeros((BLK, BLK), F32)
             for l in range(DIAG_LEVELS):
                 mix = jnp.where(lev == l, wsc[h, l:l + 1, cols], mix)
-            scores = mm(k_ref[cols, h * 128:h * 128 + 128], qt[h, :, cols])
+            scores = mm(kn[h, cols, :], qt[h, :, cols])
             weighted = (mix * scores).astype(BF16)
             st_ref[h, b] = scores
             mix_ref[h, b] = mix
@@ -210,9 +248,6 @@
         left_msgs[u].wait_recv()
         summed[1, u] = (pf[1, u] + r1[1, u].astype(F32)).astype(BF16)
         send_left(4 + u, summed.at[1, u], rdir.at[1, 1, u])
-    take_states(2)
-    if dev_bits > 3:
-        send_states(3)
 
     for h in range(2):
         for slot, (c, first, size) in enumerate(LOCAL_PAIRS):
@@ -226,16 +261,13 @@
             part = partial_grad(0, u, j)
             pf[0, u, :, at] = part[:128]
             pf[1, u, :, at] = part[128:]
-    for step in range(3, dev_bits):
-        take_states(step)
-        if step + 1 < dev_bits:
-            send_states(step + 1)
+    take_states(2)
 
     @pl.loop(0, 8)
     def _(b):
         cols = cols_of(b)
         for h in range(2):
-            far = mm(tstt[h], wq[h, 3:, :, cols].reshape(dev_bits * 128, BLK))
+            far = mm(tstt[h], wq[h, 3:, :, cols].reshape(DEV_BITS * 128, BLK))
             hall[0, cols, h * 128:h * 128 + 128] = (ot[h, :, cols] + far).T.astype(BF16)
 
     h_copies = {}
@@ -259,30 +291,40 @@
             gt[h, :, at] = (pf[h, u] + rdir[0, h, u].astype(F32) + rdir[1, h, u].astype(F32)).astype(BF16)
 
     for h in range(2):
-        grads = mm_nt(wq[h, 3:].reshape(dev_bits * 128, 1024), gt[h])
-        for step in range(dev_bits):
+        grads = mm_nt(wq[h, 3:].reshape(DEV_BITS * 128, 1024), gt[h])
+        for step in range(DEV_BITS):
             lg[h, step] = grads[step * 128:step * 128 + 128]
         xf[h] = jnp.zeros((128, 128), F32)
 
     c_copies = {}
 
-    def send_grads(step):
-        to, has = partner(step)
-        for h in range(2):
-            cb[step, h] = (xf[h] + lg[h, step] * has.astype(F32)).astype(BF16)
-        c_copies[step] = send(cb.at[step], rcb.at[step], c_send.at[step], c_recv.at[step], to, me_h)
-
-    def take_grads(step):
-        c_copies[step].wait_recv()
-        for h in range(2):
-            xf[h] = xf[h] + rcb[step, h].astype(F32)
+    def send_grads(phase):
+        for h in range(2):
+            if phase == 0:
+                cb[0, h] = (xf[h] + lg[h, 0] * bit_of(0).astype(F32)).astype(BF16)
+            else:
+                for i in range(2):
+                    slot = 2 * phase - 1 + i
+                    cb[slot, h] = (xf[h] + lg[h, slot] * bit_of(slot).astype(F32)).astype(BF16)
+        for n, step in enumerate(PHASES[phase]):
+            slot = 2 * phase - 1 + min(n, 1) if phase else 0
+            c_copies[step] = send(cb.at[slot], rcb.at[step], c_send.at[step], c_recv.at[step], partner(step), me_h)
+
+    def take_grads(phase):
+        for step in PHASES[phase]:
+            c_copies[step].wait_recv()
+        for h in range(2):
+            total_grad = xf[h]
+            for step in PHASES[phase]:
+                total_grad = total_grad + rcb[step, h].astype(F32)
+            xf[h] = total_grad
 
     def diag_backward(b):
         cols = cols_of(b)
         for h in range(2):
             lev = lev_ref[...]
             gb = gt[h, :, cols]
-            grad_scores = mm(v_ref[cols, h * 128:h * 128 + 128], gb)
+            grad_scores = mm(vn[h, cols, :], gb)
             weighted = (mix_ref[h, b] * grad_scores).astype(BF16)
             product = grad_scores * st_ref[h, b]
             dqa[h, :, cols] = mm(kt[h, :, cols], weighted)
@@ -298,9 +340,10 @@
             gb = gt[h, :, cols]
             qf = qt[h, :, cols].astype(F32)
             sums = dqa[h, :, cols]
-            for step in range(dev_bits):
+            all_got = mm(tst[h], gb)
+            for step in range(DEV_BITS):
                 l = LOCAL_LEVELS + step
-                got = mm(tst[h, step], gb)
+                got = all_got[step * 128:step * 128 + 128]
                 sums = sums + got * wsc[h, l:l + 1, cols]
                 wg_ref[l, h:h + 1, cols] = jnp.sum(got * qf, axis=0, keepdims=True) * scale_of(l)
             dqa[h, :, cols] = sums
@@ -317,35 +360,40 @@
             wg_ref[l, h:h + 1, at] = jnp.sum(got * qt[h, :, at].astype(F32), axis=0, keepdims=True) * scale_of(l)
             llg[h, slot] = mm_nt(wq[h, c, :, at], gb)
 
-    work = [
-        lambda: pl.loop(0, 4)(diag_backward),
-        lambda: pl.loop(4, 8)(diag_backward),
-        lambda: pl.loop(0, 4)(far_backward),
-        lambda: pl.loop(4, 8)(far_backward),
-        lambda: [local_backward(h) for h in range(2)],
-    ]
-    relayed = 0
-    for step in reversed(range(dev_bits)):
-        send_grads(step)
-        if work:
-            work.pop(0)()
-        take_grads(step)
-        if step == dev_bits - 2:
-            h_copies[0].wait_recv()
-            send_heads(4, 1, 0, 2, right)
-            h_copies[1].wait_recv()
-            send_heads(5, 3, 1, 2, left)
-    for item in work:
-        item()
+    send_grads(2)
+    pl.loop(0, 8)(diag_backward)
+    take_grads(2)
+    send_grads(1)
+    pl.loop(0, 8)(far_backward)
+    h_copies[0].wait_recv()
+    send_heads(4, 1, 0, 2, right)
+    h_copies[1].wait_recv()
+    send_heads(5, 3, 1, 2, left)
+    take_grads(1)
+    send_grads(0)
+    for h in range(2):
+        local_backward(h)
+
+    stores = []
+
+    def store(src, dst):
+        stores.append(pltpu.make_async_copy(src, dst, out_sem.at[len(stores)]))
+        stores[-1].start()
+
+    store(wg_ref, wg_out)
 
     @pl.loop(0, 8)
     def _(b):
         cols = cols_of(b)
-        for h in range(2):
-            dq_ref[cols, h * 128:h * 128 + 128] = dqa[h, :, cols].T.astype(BF16)
+        both = jnp.concatenate([dqa[h, :, cols].T.astype(BF16) for h in range(2)], axis=1)
+        dq_ref[cols] = both.reshape(BLK, 2, 128)
+
+    store(dq_ref, dq_out)
+    take_grads(0)
 
     for b in range(8):
         at = slice(b * BLK, b * BLK + BLK)
+        dks, dvs = [], []
         for h in range(2):
             x = xf[h]
             for slot, (c, first, size) in enumerate(LOCAL_PAIRS):
@@ -353,8 +401,13 @@
                     x = x + llg[h, slot]
             dk = dka[h, :, at] + mm(x.astype(BF16), vt[h, :, at])
             dv = dva[h, :, at] + mm(x.T.astype(BF16), kt[h, :, at])
-            dk_ref[at, h * 128:h * 128 + 128] = dk.T.astype(BF16)
-            dv_ref[at, h * 128:h * 128 + 128] = dv.T.astype(BF16)
+            dks.append(dk.T.astype(BF16))
+            dvs.append(dv.T.astype(BF16))
+        dk_ref[at] = jnp.concatenate(dks, axis=1).reshape(BLK, 2, 128)
+        dv_ref[at] = jnp.concatenate(dvs, axis=1).reshape(BLK, 2, 128)
+
+    store(dk_ref, dk_out)
+    store(dv_ref, dv_out)
 
     @pl.loop(0, 4)
     def _(b):
@@ -369,41 +422,57 @@
         rows = pl.ds(pl.multiple_of(b * 256, 256), 256)
         acc[rows, :] = acc[rows, :] + mm(hall[1, rows, :], wall[1]) + mm(hall[3, rows, :], wall[3])
 
-    h_copies[4].wait_recv()
-    h_copies[5].wait_recv()
-
-    @pl.loop(0, 4)
-    def _(b):
-        rows = pl.ds(pl.multiple_of(b * 256, 256), 256)
-        lo_ref[rows, :] = (acc[rows, :] + mm(hall[2, rows, :], wall[2])).astype(BF16)
-
-    for group in (w_copies, f_copies, right_msgs, left_msgs, h_copies, c_copies):
+    for part in range(2):
+        h_copies[4 + part].wait_recv()
+        for b in range(2 * part, 2 * part + 2):
+            rows = slice(b * 256, b * 256 + 256)
+            lo_ref[rows, :] = (acc[rows, :] + mm(hall[2, rows, :], wall[2])).astype(BF16)
+            store(lo_ref.at[rows], lo_out.at[rows])
+
+    for group in (w_copies, f_copies, right_msgs, left_msgs, h_copies, b_copies, c_copies):
         for copy in group.values():
             copy.wait_send()
-    for copy in b_copies:
-        copy.wait_send()
+    for copy in stores:
+        copy.wait()
+
+
+def copy_kernel(*refs):
+    sources, targets, sems = refs[:5], refs[5:10], refs[10]
+    copies = [pltpu.make_async_copy(a, b, sems.at[i]) for i, (a, b) in enumerate(zip(sources, targets))]
+    for copy in copies:
+        copy.start()
+    for copy in copies:
+        copy.wait()
 
 
 def per_device(queries, key_rows, value_rows, level_weights, out_weight, out_grad):
-    dev_bits = lax.axis_size("seq").bit_length() - 1
     dma = pltpu.SemaphoreType.DMA
     vmem = pltpu.VMEM
-    full = pl.BlockSpec(memory_space=pltpu.VMEM)
-    stack = 3 + dev_bits
+    anywhere = pl.BlockSpec(memory_space=pl.ANY)
+    hbm = pl.BlockSpec(memory_space=pltpu.HBM)
+    stack = 3 + DEV_BITS
+    shape = queries.shape
+    shapes = (
+        jax.ShapeDtypeStruct(out_grad.shape, BF16),
+        jax.ShapeDtypeStruct(shape, BF16),
+        jax.ShapeDtypeStruct(shape, BF16),
+        jax.ShapeDtypeStruct(shape, BF16),
+        jax.ShapeDtypeStruct(level_weights.shape, F32),
+    )
     outs = pl.pallas_call(
-        functools.partial(kernel, dev_bits),
-        out_shape=(
-            jax.ShapeDtypeStruct((1024, 512), BF16),
-            jax.ShapeDtypeStruct((1024, 256), BF16),
-            jax.ShapeDtypeStruct((1024, 256), BF16),
-            jax.ShapeDtypeStruct((1024, 256), BF16),
-            jax.ShapeDtypeStruct(level_weights.shape, F32),
-        ),
-        in_specs=[full, full, full, full, pl.BlockSpec(memory_space=pl.ANY), full],
-        out_specs=[full] * 5,
+        kernel,
+        out_shape=shapes,
+        in_specs=[hbm] * 6,
+        out_specs=[anywhere] * 5,
         scratch_shapes=[
+            vmem(shape, BF16), vmem(shape, BF16), vmem(shape, BF16),
+            vmem(level_weights.shape, F32), vmem(out_grad.shape, BF16),
+            vmem(out_grad.shape, BF16),
+            vmem(shape, BF16), vmem(shape, BF16), vmem(shape, BF16),
+            vmem(level_weights.shape, F32),
+            vmem((2, 1024, 128), BF16), vmem((2, 1024, 128), BF16),
             vmem((4, 256, 512), BF16),
-            vmem((2, LOCAL_LEVELS + dev_bits, 1024), F32),
+            vmem((2, LOCAL_LEVELS + DEV_BITS, 1024), F32),
             vmem((BLK, BLK), jnp.int32),
             vmem((2, 128, 1024), BF16),
             vmem((2, 128, 1024), BF16),
@@ -417,13 +486,13 @@
             vmem((2, 7, 128, 128), BF16),
             vmem((2, 7, 128, 128), BF16),
             vmem((2, 128, 1024), F32),
-            vmem((dev_bits, 2, 128, 128), BF16),
-            vmem((dev_bits, 2, 128, 128), BF16),
-            vmem((dev_bits, 2, 128, 128), BF16),
-            vmem((dev_bits, 2, 128, 128), BF16),
-            vmem((2, dev_bits, 128, 128), BF16),
-            vmem((2, 128, dev_bits * 128), BF16),
-            vmem((2, dev_bits, 128, 128), F32),
+            vmem((3, 2, 128, 128), BF16),
+            vmem((7, 2, 128, 128), BF16),
+            vmem((5, 2, 128, 128), BF16),
+            vmem((7, 2, 128, 128), BF16),
+            vmem((2, DEV_BITS * 128, 128), BF16),
+            vmem((2, 128, DEV_BITS * 128), BF16),
+            vmem((2, DEV_BITS, 128, 128), F32),
             vmem((2, 128, 128), F32),
             vmem((2, 7, 128, 128), F32),
             vmem((2, 2, 128, 512), BF16),
@@ -437,21 +506,27 @@
             vmem((2, 128, 1024), F32),
             vmem((2, 128, 1024), F32),
             vmem((1024, 512), F32),
-            dma,
+            dma((5,)), dma((8,)), dma,
             dma((3,)), dma((3,)), dma((3,)), dma((3,)),
-            dma((dev_bits,)), dma((dev_bits,)), dma((dev_bits,)), dma((dev_bits,)),
+            dma((7,)), dma((7,)), dma((7,)), dma((7,)),
             dma((12,)), dma((12,)), dma((6,)), dma((6,)),
         ],
         compiler_params=pltpu.CompilerParams(
-            collective_id=0, has_side_effects=True, vmem_limit_bytes=56 * 1024 * 1024),
+            collective_id=0, has_side_effects=True, vmem_limit_bytes=40 * 1024 * 1024),
         cost_estimate=pl.CostEstimate(flops=6 * 10**9, bytes_accessed=8 * 2**20, transcendentals=0),
     )(
-        queries.reshape(1024, 256), key_rows.reshape(1024, 256), value_rows.reshape(1024, 256),
-        level_weights, out_weight.reshape(256, 2048), out_grad,
+        *(pltpu.with_memory_space_constraint(x, pltpu.HBM) for x in (
+            queries, key_rows, value_rows, level_weights, out_weight.reshape(256, 2048), out_grad)),
     )
-    layer_out, dq, dk, dv, wg = outs
-    shape = queries.shape
-    return layer_out, dq.reshape(shape), dk.reshape(shape), dv.reshape(shape), wg
+    return pl.pallas_call(
+        copy_kernel,
+        out_shape=shapes,
+        in_specs=[anywhere] * 5,
+        out_specs=[hbm] * 5,
+        scratch_shapes=[dma((5,))],
+        compiler_params=pltpu.CompilerParams(vmem_limit_bytes=2 * 1024 * 1024),
+        cost_estimate=pl.CostEstimate(flops=0, bytes_accessed=6 * 2**20, transcendentals=0),
+    )(*outs)
 
 
 def solution(mesh):

time: 71.8 us -> 56.6 us (0.79)
  local copies, waits for them, and re-layouts: 8.7 us -> 0 us
  Pallas kernels: 62.3 us -> 55.9 us
    pallas_call x1 -> x2, Pallas kernels: 62.3 us -> 55.9 us  [the longest x1 54.3 us: per_device(): pl.pallas_call(kernel, out_shape=shapes, in_specs=[hbm] * 6, out_specs=[a...]
    reshape x4 -> x0, local copies, waits for them, and re-layouts: 5 us -> none  [the longest x1 2.04 us: per_device(): dq.reshape(shape)]
    unnamed x15 -> x0, local copies, waits for them, and re-layouts: 3.7 us -> none
where the time goes in v1:
time: 56.6 us; the launch traced here: 56.5 us
  Pallas kernels  55.9 us (99%)
  between operations  0.64 us (1%)
    pallas_call x1, Pallas kernels, per_device(): pl.pallas_call(kernel, out_shape=shapes, in_specs=[hbm] * 6, out_specs=[a...  54.3 us
    pallas_call x1, Pallas kernels, per_device(): pl.pallas_call(copy_kernel, out_shape=shapes, in_specs=[anywhere] * 5, ou...  1.56 us

profile of v1, /device:TPU:1, one launch (start us, length us, event | category | flops | bytes accessed | tf_op | source)
XLA Modules:
  0.0 56.5 jit_solution(8761369949212956670)
XLA Ops:
  0.6 54.3 %shard_map.101 = (bf16[1024,512]{1,0:T(8,128)(2,1)S(1)}, bf16[1024,2,128]{2,1,0:T(2,128)(2,1)S(1)}, bf16[1024,2,128]{2,1,0:T(2,128)(2,1)S(1)}, bf16[1024,2,128]{2,1,0:T(2,128)(2,1)S(1)}, f32[16,2,1024]{2,1,0:T(2,128)S(1)}) custom-call(bf16[1024,2,128]{2,1,0:T(2,128)(2,1)} %q_in.1, bf16[1024,2,128]{2,1,0:T(2,128)(2,1)} %k_in.1, bf16[1024,2,128]{2,1,0:T(2,128)(2,1)} %v_in.1, ...), custom_call_target="tpu_custom_call" | custom-call | flops 6000000000 | bytes 8388608 | tf_op jit(solution)/shard_map/pallas_call | solution.py:462
  54.9 1.6 %shard_map.102 = (bf16[1024,512]{1,0:T(8,128)(2,1)}, bf16[1024,2,128]{2,1,0:T(2,128)(2,1)}, bf16[1024,2,128]{2,1,0:T(2,128)(2,1)}, bf16[1024,2,128]{2,1,0:T(2,128)(2,1)}, f32[16,2,1024]{2,1,0:T(2,128)}) custom-call(bf16[1024,512]{1,0:T(8,128)(2,1)S(1)} %get-tuple-element.10.refs_0_, bf16[1024,2,128]{2,1,0:T(2,128)(2,1)S(1)} %get-tuple-element.11.refs_1_, ...), custom_call_target="tpu_custom_call" | custom-call | bytes 6291456 | tf_op jit(solution)/shard_map/pallas_call | solution.py:521

commit v2 on v1

--- a/solution.py
+++ b/solution.py
@@ -39,7 +39,7 @@
     q_ref, k_ref, v_ref, lw_ref, og_ref, lo_ref, dq_ref, dk_ref, dv_ref, wg_ref, kn, vn,
     wall, wsc, lev_ref, qt, kt, vt, gt, wq, st_ref, mix_ref, near, tb, tl, tlt, ot,
     sb, rb, cb, rcb, tst, tstt, lg, xf, llg,
-    p2, alone, pf, summed, r1, rdir, hall, dqa, dka, dva, acc,
+    p2, alone, pf, po, summed, r1, rdir, hall, dqa, dka, dva, acc,
     in_sem, out_sem, own_sem, w_send, w_recv, f_send, f_recv, b_send, b_recv, c_send, c_recv, r_send, r_recv, h_send, h_recv,
 ):
     me_s = lax.axis_index("seq")
@@ -112,7 +112,7 @@
     loads[0].wait()
     loads[1].wait()
 
-    @pl.loop(0, 8)
+    @pl.loop(0, 8, unroll=4)
     def _(b):
         cols = cols_of(b)
         k_all, v_all = k_ref[cols].reshape(BLK, 256), v_ref[cols].reshape(BLK, 256)
@@ -163,7 +163,6 @@
                 xf[h] = xf[h] + got[0] + far
 
     send_states(0)
-    forward_weights(2)
     loads[2].wait()
     loads[3].wait()
 
@@ -171,7 +170,10 @@
         for l in range(LOCAL_LEVELS + DEV_BITS):
             wsc[h, l:l + 1, :] = lw_ref[l, h:h + 1, :] * scale_of(l)
 
-    @pl.loop(0, 8)
+    take_states(0)
+    send_states(1)
+
+    @pl.loop(0, 8, unroll=4)
     def _(b):
         cols = cols_of(b)
         q_all = q_ref[cols].reshape(BLK, 256)
@@ -194,20 +196,26 @@
         rows = slice(u * 512 + j * 256, u * 512 + j * 256 + 256)
         return mm_nt(wall[k], og_ref[rows, :])
 
-    take_states(0)
-    send_states(1)
     loads[4].wait()
+    forward_weights(2)
+    started = []
+
+    def first_leg(head, to):
+        rows = pl.ds(pl.multiple_of(head * 128, 128), 128)
+        for u in range(2):
+            p2[head, u] = mm_nt(wall[2, rows, :], og_ref[u * 512:u * 512 + 512, :]).astype(BF16)
+            started.append(send(
+                p2.at[head, u], r1.at[head, u], r_send.at[6 * head + u], r_recv.at[6 * head + u], me_s, to))
+
+    def await_first(head, u):
+        pltpu.make_async_remote_copy(
+            src_ref=p2.at[head, u], dst_ref=r1.at[head, u], send_sem=r_send.at[6 * head + u],
+            recv_sem=r_recv.at[6 * head + u], device_id=(me_s, left), device_id_type=MESH,
+        ).wait_recv()
+
+    first_leg(core, lax.rem(me_h + 1 + 2 * core, 4))
     f_copies[2].wait_recv()
-    for u in range(2):
-        for j in range(2):
-            part = partial_grad(2, u, j).astype(BF16)
-            p2[0, u, :, j * 256:j * 256 + 256] = part[:128]
-            p2[1, u, :, j * 256:j * 256 + 256] = part[128:]
-        send_right(u, p2.at[0, u], r1.at[0, u])
-        send_left(u, p2.at[1, u], r1.at[1, u])
-
-    forward_weights(1)
-    forward_weights(3)
+    first_leg(1 - core, lax.rem(me_h + 3 - 2 * core, 4))
 
     def diag_forward(b):
         cols = cols_of(b)
@@ -223,7 +231,11 @@
             near[h, b] = weighted
             ot[h, :, cols] = mm(vt[h, :, cols], weighted)
 
-    pl.loop(0, 4)(diag_forward)
+    pl.loop(0, 4, unroll=4)(diag_forward)
+    forward_weights(1)
+    forward_weights(3)
+    take_states(1)
+    send_states(2)
     f_copies[1].wait_recv()
     f_copies[3].wait_recv()
     for u in range(2):
@@ -237,17 +249,7 @@
             pf[1, u, :, at] = part[128:]
         send_right(2 + u, alone.at[0, u], rdir.at[0, 1, u])
         send_left(2 + u, alone.at[1, u], rdir.at[1, 0, u])
-    take_states(1)
-    send_states(2)
-    pl.loop(4, 8)(diag_forward)
-
-    for u in range(2):
-        right_msgs[u].wait_recv()
-        summed[0, u] = (pf[0, u] + r1[0, u].astype(F32)).astype(BF16)
-        send_right(4 + u, summed.at[0, u], rdir.at[0, 0, u])
-        left_msgs[u].wait_recv()
-        summed[1, u] = (pf[1, u] + r1[1, u].astype(F32)).astype(BF16)
-        send_left(4 + u, summed.at[1, u], rdir.at[1, 1, u])
+    pl.loop(4, 8, unroll=4)(diag_forward)
 
     for h in range(2):
         for slot, (c, first, size) in enumerate(LOCAL_PAIRS):
@@ -259,11 +261,19 @@
         for j in range(2):
             at = slice(j * 256, j * 256 + 256)
             part = partial_grad(0, u, j)
-            pf[0, u, :, at] = part[:128]
-            pf[1, u, :, at] = part[128:]
+            po[0, u, :, at] = part[:128]
+            po[1, u, :, at] = part[128:]
+    for u in range(2):
+        await_first(0, u)
+        summed[0, u] = (pf[0, u] + r1[0, u].astype(F32)).astype(BF16)
+        send_right(4 + u, summed.at[0, u], rdir.at[0, 0, u])
+        await_first(1, u)
+        summed[1, u] = (pf[1, u] + r1[1, u].astype(F32)).astype(BF16)
+        send_left(4 + u, summed.at[1, u], rdir.at[1, 1, u])
+
     take_states(2)
 
-    @pl.loop(0, 8)
+    @pl.loop(0, 8, unroll=4)
     def _(b):
         cols = cols_of(b)
         for h in range(2):
@@ -272,28 +282,35 @@
 
     h_copies = {}
 
-    def send_heads(i, slot, part, to_slot, head):
-        rows = slice(part * 512, part * 512 + 512)
+    def send_heads(i, slot, piece, to_slot, head):
+        rows = slice(piece * 256, piece * 256 + 256)
         h_copies[i] = send(hall.at[slot, rows], hall.at[to_slot, rows], h_send.at[i], h_recv.at[i], me_s, head)
 
-    send_heads(0, 0, 0, 1, right)
-    send_heads(1, 0, 1, 3, left)
-    send_heads(2, 0, 1, 1, right)
-    send_heads(3, 0, 0, 3, left)
-
-    for u in range(2):
+    for n in range(4):
+        send_heads(n, 0, n, 1, right)
+        send_heads(6 + n, 0, (n + 2) % 4, 3, left)
+
+    def relay_heads(n):
+        h_copies[n].wait_recv()
+        send_heads(4 + n, 1, n, 2, right)
+        h_copies[6 + n].wait_recv()
+        send_heads(10 + n, 3, n + 2, 2, left)
+
+    def take_head_grad(u):
         at = slice(u * 512, u * 512 + 512)
         right_msgs[2 + u].wait_recv()
         left_msgs[2 + u].wait_recv()
         right_msgs[4 + u].wait_recv()
         left_msgs[4 + u].wait_recv()
         for h in range(2):
-            gt[h, :, at] = (pf[h, u] + rdir[0, h, u].astype(F32) + rdir[1, h, u].astype(F32)).astype(BF16)
+            gt[h, :, at] = (po[h, u] + rdir[0, h, u].astype(F32) + rdir[1, h, u].astype(F32)).astype(BF16)
+        for h in range(2):
+            grads = mm_nt(wq[h, 3:, :, at].reshape(DEV_BITS * 128, 512), gt[h, :, at])
+            for step in range(DEV_BITS):
+                piece = grads[step * 128:step * 128 + 128]
+                lg[h, step] = piece if u == 0 else lg[h, step] + piece
 
     for h in range(2):
-        grads = mm_nt(wq[h, 3:].reshape(DEV_BITS * 128, 1024), gt[h])
-        for step in range(DEV_BITS):
-            lg[h, step] = grads[step * 128:step * 128 + 128]
         xf[h] = jnp.zeros((128, 128), F32)
 
     c_copies = {}
@@ -360,17 +377,17 @@
             wg_ref[l, h:h + 1, at] = jnp.sum(got * qt[h, :, at].astype(F32), axis=0, keepdims=True) * scale_of(l)
             llg[h, slot] = mm_nt(wq[h, c, :, at], gb)
 
+    take_head_grad(0)
+    pl.loop(0, 4, unroll=4)(diag_backward)
+    take_head_grad(1)
     send_grads(2)
-    pl.loop(0, 8)(diag_backward)
+    pl.loop(0, 4, unroll=4)(far_backward)
+    pl.loop(4, 8, unroll=4)(diag_backward)
+    relay_heads(0)
+    relay_heads(1)
     take_grads(2)
     send_grads(1)
-    pl.loop(0, 8)(far_backward)
-    h_copies[0].wait_recv()
-    send_heads(4, 1, 0, 2, right)
-    h_copies[1].wait_recv()
-    send_heads(5, 3, 1, 2, left)
-    take_grads(1)
-    send_grads(0)
+    pl.loop(4, 8, unroll=4)(far_backward)
     for h in range(2):
         local_backward(h)
 
@@ -382,13 +399,30 @@
 
     store(wg_ref, wg_out)
 
-    @pl.loop(0, 8)
+    @pl.loop(0, 8, unroll=4)
     def _(b):
         cols = cols_of(b)
         both = jnp.concatenate([dqa[h, :, cols].T.astype(BF16) for h in range(2)], axis=1)
         dq_ref[cols] = both.reshape(BLK, 2, 128)
 
     store(dq_ref, dq_out)
+
+    @pl.loop(0, 4, unroll=2)
+    def _(b):
+        rows = pl.ds(pl.multiple_of(b * 256, 256), 256)
+        acc[rows, :] = mm(hall[0, rows, :], wall[0])
+
+    take_grads(1)
+    send_grads(0)
+    for n in (2, 3):
+        h_copies[n].wait_recv()
+        h_copies[6 + n].wait_recv()
+
+    @pl.loop(0, 4, unroll=2)
+    def _(b):
+        rows = pl.ds(pl.multiple_of(b * 256, 256), 256)
+        acc[rows, :] = acc[rows, :] + mm(hall[1, rows, :], wall[1]) + mm(hall[3, rows, :], wall[3])
+
     take_grads(0)
 
     for b in range(8):
@@ -409,22 +443,9 @@
     store(dk_ref, dk_out)
     store(dv_ref, dv_out)
 
-    @pl.loop(0, 4)
-    def _(b):
-        rows = pl.ds(pl.multiple_of(b * 256, 256), 256)
-        acc[rows, :] = mm(hall[0, rows, :], wall[0])
-
-    h_copies[2].wait_recv()
-    h_copies[3].wait_recv()
-
-    @pl.loop(0, 4)
-    def _(b):
-        rows = pl.ds(pl.multiple_of(b * 256, 256), 256)
-        acc[rows, :] = acc[rows, :] + mm(hall[1, rows, :], wall[1]) + mm(hall[3, rows, :], wall[3])
-
-    for part in range(2):
-        h_copies[4 + part].wait_recv()
-        for b in range(2 * part, 2 * part + 2):
+    for n in range(2):
+        for i, b in ((4 + n, n), (10 + n, n + 2)):
+            h_copies[i].wait_recv()
             rows = slice(b * 256, b * 256 + 256)
             lo_ref[rows, :] = (acc[rows, :] + mm(hall[2, rows, :], wall[2])).astype(BF16)
             store(lo_ref.at[rows], lo_out.at[rows])
@@ -432,6 +453,8 @@
     for group in (w_copies, f_copies, right_msgs, left_msgs, h_copies, b_copies, c_copies):
         for copy in group.values():
             copy.wait_send()
+    for copy in started:
+        copy.wait_send()
     for copy in stores:
         copy.wait()
 
@@ -498,6 +521,7 @@
             vmem((2, 2, 128, 512), BF16),
             vmem((2, 2, 128, 512), BF16),
             vmem((2, 2, 128, 512), F32),
+            vmem((2, 2, 128, 512), F32),
             vmem((2, 2, 128, 512), BF16),
             vmem((2, 2, 128, 512), BF16),
             vmem((2, 2, 2, 128, 512), BF16),
@@ -509,7 +533,7 @@
             dma((5,)), dma((8,)), dma,
             dma((3,)), dma((3,)), dma((3,)), dma((3,)),
             dma((7,)), dma((7,)), dma((7,)), dma((7,)),
-            dma((12,)), dma((12,)), dma((6,)), dma((6,)),
+            dma((12,)), dma((12,)), dma((12,)), dma((12,)),
         ],
         compiler_params=pltpu.CompilerParams(
             collective_id=0, has_side_effects=True, vmem_limit_bytes=40 * 1024 * 1024),

time: 56.6 us -> 53.4 us (0.943)
  Pallas kernels: 55.9 us -> 52.7 us
    pallas_call x1, Pallas kernels: 54.3 us -> 51.1 us  [per_device(): pl.pallas_call(kernel, out_shape=shapes, in_specs=[hbm] * 6, out_specs=[a...]
where the time goes in v2:
time: 53.4 us; the launch traced here: 53.3 us
  Pallas kernels  52.7 us (99%)
  between operations  0.64 us (1%)
    pallas_call x1, Pallas kernels, per_device(): pl.pallas_call(kernel, out_shape=shapes, in_specs=[hbm] * 6, out_specs=[a...  51.1 us
    pallas_call x1, Pallas kernels, per_device(): pl.pallas_call(copy_kernel, out_shape=shapes, in_specs=[anywhere] * 5, ou...  1.56 us

profile of v2, /device:TPU:1, one launch (start us, length us, event | category | flops | bytes accessed | tf_op | source)
XLA Modules:
  0.0 53.3 jit_solution(4416208985992894011)
XLA Ops:
  0.6 51.1 %shard_map.101 = (bf16[1024,512]{1,0:T(8,128)(2,1)S(1)}, bf16[1024,2,128]{2,1,0:T(2,128)(2,1)S(1)}, bf16[1024,2,128]{2,1,0:T(2,128)(2,1)S(1)}, bf16[1024,2,128]{2,1,0:T(2,128)(2,1)S(1)}, f32[16,2,1024]{2,1,0:T(2,128)S(1)}) custom-call(bf16[1024,2,128]{2,1,0:T(2,128)(2,1)} %q_in.1, bf16[1024,2,128]{2,1,0:T(2,128)(2,1)} %k_in.1, bf16[1024,2,128]{2,1,0:T(2,128)(2,1)} %v_in.1, ...), custom_call_target="tpu_custom_call" | custom-call | flops 6000000000 | bytes 8388608 | tf_op jit(solution)/shard_map/pallas_call | solution.py:485
  51.7 1.6 %shard_map.102 = (bf16[1024,512]{1,0:T(8,128)(2,1)}, bf16[1024,2,128]{2,1,0:T(2,128)(2,1)}, bf16[1024,2,128]{2,1,0:T(2,128)(2,1)}, bf16[1024,2,128]{2,1,0:T(2,128)(2,1)}, f32[16,2,1024]{2,1,0:T(2,128)}) custom-call(bf16[1024,512]{1,0:T(8,128)(2,1)S(1)} %get-tuple-element.10.refs_0_, bf16[1024,2,128]{2,1,0:T(2,128)(2,1)S(1)} %get-tuple-element.11.refs_1_, ...), custom_call_target="tpu_custom_call" | custom-call | bytes 6291456 | tf_op jit(solution)/shard_map/pallas_call | solution.py:545

commit v3 on v2

--- a/solution.py
+++ b/solution.py
@@ -40,7 +40,7 @@
     wall, wsc, lev_ref, qt, kt, vt, gt, wq, st_ref, mix_ref, near, tb, tl, tlt, ot,
     sb, rb, cb, rcb, tst, tstt, lg, xf, llg,
     p2, alone, pf, po, summed, r1, rdir, hall, dqa, dka, dva, acc,
-    in_sem, out_sem, own_sem, w_send, w_recv, f_send, f_recv, b_send, b_recv, c_send, c_recv, r_send, r_recv, h_send, h_recv,
+    in_sem, out_sem, own_sem, w_send, w_recv, z_send, z_recv, f_send, f_recv, b_send, b_recv, c_send, c_recv, r_send, r_recv, h_send, h_recv,
 ):
     me_s = lax.axis_index("seq")
     me_h = lax.axis_index("head")
@@ -83,20 +83,46 @@
     pl.semaphore_wait(barrier, 10)
 
     own = pltpu.make_async_copy(w_hbm.at[:, pl.ds(pl.multiple_of(me_h * 512, 512), 512)], wall.at[0], own_sem)
-    half = pl.ds(pl.multiple_of(core * 128, 128), 128)
+    def rows_at(start, size):
+        return pl.ds(pl.multiple_of(start, 32), size)
+
+    def columns_of(k):
+        return pl.ds(pl.multiple_of(lax.rem(me_h + k, 4) * 512, 512), 512)
+
+    half = rows_at(core * 128, 128)
+    eighth = rows_at(core * 128 + lax.div(me_s, 8) * 32, 32)
     w_copies = {}
-    for k in (2, 1, 3):
-        to = lax.rem(me_h + k, 4)
-        w_copies[k] = send(
-            w_hbm.at[half, pl.ds(pl.multiple_of(to * 512, 512), 512)], wall.at[k, half],
-            w_send.at[k - 1], w_recv.at[k - 1], me_s, to)
+
+    def send_weights(i, k, rows):
+        w_copies[i] = send(
+            w_hbm.at[rows, columns_of(k)], wall.at[k, rows], w_send.at[i], w_recv.at[i], me_s, lax.rem(me_h + k, 4))
+
+    send_weights(0, 2, rows_at(core * 128, 64))
+    send_weights(2, 1, eighth)
+    send_weights(3, 3, eighth)
+    send_weights(1, 2, rows_at(core * 128 + 64, 64))
     own.start()
     sibling = partner(0)
     f_copies = {}
 
-    def forward_weights(k):
-        w_copies[k].wait_recv()
-        f_copies[k] = send(wall.at[k, half], wall.at[k, half], f_send.at[k - 1], f_recv.at[k - 1], sibling, me_h)
+    def to_sibling(i, k, rows):
+        f_copies[i] = send(wall.at[k, rows], wall.at[k, rows], f_send.at[i], f_recv.at[i], sibling, me_h)
+
+    z_copies = []
+
+    def share_weights():
+        for i, k in enumerate((1, 3)):
+            w_copies[2 + i].wait_recv()
+            for n in range(3):
+                at = 3 * i + n
+                z_copies.append(send(
+                    wall.at[k, eighth], wall.at[k, eighth], z_send.at[at], z_recv.at[at], partner(4 + n), me_h))
+
+    def forward_shared():
+        for i, k in enumerate((1, 3)):
+            for n in range(3):
+                z_copies[3 * i + n].wait_recv()
+            to_sibling(2 + i, k, half)
 
     row_id = lax.broadcasted_iota(jnp.int32, (BLK, BLK), 0)
     col_id = lax.broadcasted_iota(jnp.int32, (BLK, BLK), 1)
@@ -196,26 +222,32 @@
         rows = slice(u * 512 + j * 256, u * 512 + j * 256 + 256)
         return mm_nt(wall[k], og_ref[rows, :])
 
+    share_weights()
     loads[4].wait()
-    forward_weights(2)
     started = []
 
-    def first_leg(head, to):
-        rows = pl.ds(pl.multiple_of(head * 128, 128), 128)
+    def first_leg(head, r, to):
+        rows = rows_at(head * 128 + r * 64, 64)
         for u in range(2):
-            p2[head, u] = mm_nt(wall[2, rows, :], og_ref[u * 512:u * 512 + 512, :]).astype(BF16)
-            started.append(send(
-                p2.at[head, u], r1.at[head, u], r_send.at[6 * head + u], r_recv.at[6 * head + u], me_s, to))
-
-    def await_first(head, u):
-        pltpu.make_async_remote_copy(
-            src_ref=p2.at[head, u], dst_ref=r1.at[head, u], send_sem=r_send.at[6 * head + u],
-            recv_sem=r_recv.at[6 * head + u], device_id=(me_s, left), device_id_type=MESH,
-        ).wait_recv()
-
-    first_leg(core, lax.rem(me_h + 1 + 2 * core, 4))
-    f_copies[2].wait_recv()
-    first_leg(1 - core, lax.rem(me_h + 3 - 2 * core, 4))
+            at = slice(u * 512, u * 512 + 512)
+            p2[head, r, :, at] = mm_nt(wall[2, rows, :], og_ref[at, :]).astype(BF16)
+        i = 6 * head + r
+        started.append(send(p2.at[head, r], r1.at[head, r], r_send.at[i], r_recv.at[i], me_s, to))
+
+    def await_first(head):
+        for r in range(2):
+            pltpu.make_async_remote_copy(
+                src_ref=p2.at[head, r], dst_ref=r1.at[head, r], send_sem=r_send.at[6 * head + r],
+                recv_sem=r_recv.at[6 * head + r], device_id=(me_s, left), device_id_type=MESH,
+            ).wait_recv()
+
+    for r in range(2):
+        w_copies[r].wait_recv()
+        to_sibling(r, 2, rows_at(core * 128 + r * 64, 64))
+        first_leg(core, r, lax.rem(me_h + 1 + 2 * core, 4))
+    for r in range(2):
+        f_copies[r].wait_recv()
+        first_leg(1 - core, r, lax.rem(me_h + 3 - 2 * core, 4))
 
     def diag_forward(b):
         cols = cols_of(b)
@@ -232,23 +264,32 @@
             ot[h, :, cols] = mm(vt[h, :, cols], weighted)
 
     pl.loop(0, 4, unroll=4)(diag_forward)
-    forward_weights(1)
-    forward_weights(3)
     take_states(1)
     send_states(2)
-    f_copies[1].wait_recv()
+    forward_shared()
+
+    def second_leg(head, k, to):
+        rows = rows_at(head * 128, 128)
+        for u in range(2):
+            alone[head, u] = mm_nt(wall[k, rows, :], og_ref[u * 512:u * 512 + 512, :]).astype(BF16)
+            i = 8 - 6 * head + u
+            started.append(send(
+                alone.at[head, u], rdir.at[head, head, u], r_send.at[i], r_recv.at[i], me_s, to))
+
+    def await_second(head, u):
+        i = 8 - 6 * head + u
+        pltpu.make_async_remote_copy(
+            src_ref=alone.at[head, u], dst_ref=rdir.at[head, head, u], send_sem=r_send.at[i], recv_sem=r_recv.at[i],
+            device_id=(me_s, left), device_id_type=MESH,
+        ).wait_recv()
+
+    second_leg(core, 1 + 2 * core, lax.rem(me_h + 3 + 2 * core, 4))
+    f_copies[2].wait_recv()
     f_copies[3].wait_recv()
+    second_leg(1 - core, 3 - 2 * core, lax.rem(me_h + 1 + 2 * core, 4))
     for u in range(2):
-        for j in range(2):
-            at = slice(j * 256, j * 256 + 256)
-            part = partial_grad(3, u, j)
-            pf[0, u, :, at] = part[:128]
-            alone[0, u, :, at] = part[128:].astype(BF16)
-            part = partial_grad(1, u, j)
-            alone[1, u, :, at] = part[:128].astype(BF16)
-            pf[1, u, :, at] = part[128:]
-        send_right(2 + u, alone.at[0, u], rdir.at[0, 1, u])
-        send_left(2 + u, alone.at[1, u], rdir.at[1, 0, u])
+        for head, k in ((0, 3), (1, 1)):
+            pf[head, u] = mm_nt(wall[k, head * 128:head * 128 + 128, :], og_ref[u * 512:u * 512 + 512, :])
     pl.loop(4, 8, unroll=4)(diag_forward)
 
     for h in range(2):
@@ -263,14 +304,16 @@
             part = partial_grad(0, u, j)
             po[0, u, :, at] = part[:128]
             po[1, u, :, at] = part[128:]
+    await_first(0)
+    await_first(1)
     for u in range(2):
-        await_first(0, u)
-        summed[0, u] = (pf[0, u] + r1[0, u].astype(F32)).astype(BF16)
-        send_right(4 + u, summed.at[0, u], rdir.at[0, 0, u])
-        await_first(1, u)
-        summed[1, u] = (pf[1, u] + r1[1, u].astype(F32)).astype(BF16)
-        send_left(4 + u, summed.at[1, u], rdir.at[1, 1, u])
-
+        at = slice(u * 512, u * 512 + 512)
+        for head in range(2):
+            for r in range(2):
+                rows = slice(r * 64, r * 64 + 64)
+                summed[head, u, rows, :] = (pf[head, u, rows, :] + r1[head, r, :, at].astype(F32)).astype(BF16)
+        send_right(4 + u, summed.at[0, u], rdir.at[1, 0, u])
+        send_left(4 + u, summed.at[1, u], rdir.at[0, 1, u])
     take_states(2)
 
     @pl.loop(0, 8, unroll=4)
@@ -298,8 +341,8 @@
 
     def take_head_grad(u):
         at = slice(u * 512, u * 512 + 512)
-        right_msgs[2 + u].wait_recv()
-        left_msgs[2 + u].wait_recv()
+        await_second(0, u)
+        await_second(1, u)
         right_msgs[4 + u].wait_recv()
         left_msgs[4 + u].wait_recv()
         for h in range(2):
@@ -450,7 +493,7 @@
             lo_ref[rows, :] = (acc[rows, :] + mm(hall[2, rows, :], wall[2])).astype(BF16)
             store(lo_ref.at[rows], lo_out.at[rows])
 
-    for group in (w_copies, f_copies, right_msgs, left_msgs, h_copies, b_copies, c_copies):
+    for group in (w_copies, f_copies, dict(enumerate(z_copies)), right_msgs, left_msgs, h_copies, b_copies, c_copies):
         for copy in group.values():
             copy.wait_send()
     for copy in started:
@@ -518,12 +561,12 @@
             vmem((2, DEV_BITS, 128, 128), F32),
             vmem((2, 128, 128), F32),
             vmem((2, 7, 128, 128), F32),
-            vmem((2, 2, 128, 512), BF16),
+            vmem((2, 2, 64, 1024), BF16),
             vmem((2, 2, 128, 512), BF16),
             vmem((2, 2, 128, 512), F32),
             vmem((2, 2, 128, 512), F32),
             vmem((2, 2, 128, 512), BF16),
-            vmem((2, 2, 128, 512), BF16),
+            vmem((2, 2, 64, 1024), BF16),
             vmem((2, 2, 2, 128, 512), BF16),
             vmem((4, 1024, 256), BF16),
             vmem((2, 128, 1024), F32),
@@ -531,7 +574,7 @@
             vmem((2, 128, 1024), F32),
             vmem((1024, 512), F32),
             dma((5,)), dma((8,)), dma,
-            dma((3,)), dma((3,)), dma((3,)), dma((3,)),
+            dma((4,)), dma((4,)), dma((6,)), dma((6,)), dma((4,)), dma((4,)),
             dma((7,)), dma((7,)), dma((7,)), dma((7,)),
             dma((12,)), dma((12,)), dma((12,)), dma((12,)),
         ],

time: 53.4 us -> 52.1 us (0.976)
  Pallas kernels: 52.7 us -> 50.8 us
    pallas_call x1, Pallas kernels: 51.1 us -> 49.3 us  [per_device(): pl.pallas_call(kernel, out_shape=shapes, in_specs=[hbm] * 6, out_specs=[a...]
where the time goes in v3:
time: 52.1 us; the launch traced here: 51.5 us
  Pallas kernels  50.8 us (98%)
  between operations  0.64 us (1%)
    pallas_call x1, Pallas kernels, per_device(): pl.pallas_call(kernel, out_shape=shapes, in_specs=[hbm] * 6, out_specs=[a...  49.3 us
    pallas_call x1, Pallas kernels, per_device(): pl.pallas_call(copy_kernel, out_shape=shapes, in_specs=[anywhere] * 5, ou...  1.56 us

profile of v3, /device:TPU:1, one launch (start us, length us, event | category | flops | bytes accessed | tf_op | source)
XLA Modules:
  0.0 51.5 jit_solution(5753689935067024792)
XLA Ops:
  0.6 49.3 %shard_map.101 = (bf16[1024,512]{1,0:T(8,128)(2,1)S(1)}, bf16[1024,2,128]{2,1,0:T(2,128)(2,1)S(1)}, bf16[1024,2,128]{2,1,0:T(2,128)(2,1)S(1)}, bf16[1024,2,128]{2,1,0:T(2,128)(2,1)S(1)}, f32[16,2,1024]{2,1,0:T(2,128)S(1)}) custom-call(bf16[1024,2,128]{2,1,0:T(2,128)(2,1)} %q_in.1, bf16[1024,2,128]{2,1,0:T(2,128)(2,1)} %k_in.1, bf16[1024,2,128]{2,1,0:T(2,128)(2,1)} %v_in.1, ...), custom_call_target="tpu_custom_call" | custom-call | flops 6000000000 | bytes 8388608 | tf_op jit(solution)/shard_map/pallas_call | solution.py:528
  49.9 1.6 %shard_map.102 = (bf16[1024,512]{1,0:T(8,128)(2,1)}, bf16[1024,2,128]{2,1,0:T(2,128)(2,1)}, bf16[1024,2,128]{2,1,0:T(2,128)(2,1)}, bf16[1024,2,128]{2,1,0:T(2,128)(2,1)}, f32[16,2,1024]{2,1,0:T(2,128)}) custom-call(bf16[1024,512]{1,0:T(8,128)(2,1)S(1)} %get-tuple-element.10.refs_0_, bf16[1024,2,128]{2,1,0:T(2,128)(2,1)S(1)} %get-tuple-element.11.refs_1_, ...), custom_call_target="tpu_custom_call" | custom-call | bytes 6291456 | tf_op jit(solution)/shard_map/pallas_call | solution.py:588

commit v4 on v3

--- a/solution.py
+++ b/solution.py
@@ -39,8 +39,8 @@
     q_ref, k_ref, v_ref, lw_ref, og_ref, lo_ref, dq_ref, dk_ref, dv_ref, wg_ref, kn, vn,
     wall, wsc, lev_ref, qt, kt, vt, gt, wq, st_ref, mix_ref, near, tb, tl, tlt, ot,
     sb, rb, cb, rcb, tst, tstt, lg, xf, llg,
-    p2, alone, pf, po, summed, r1, rdir, hall, dqa, dka, dva, acc,
-    in_sem, out_sem, own_sem, w_send, w_recv, z_send, z_recv, f_send, f_recv, b_send, b_recv, c_send, c_recv, r_send, r_recv, h_send, h_recv,
+    p2, alone, pf, po, summed, r1, ra, rb_sum, hall, dqa, dka, dva, acc,
+    in_sem, out_sem, own_sem, w_send, w_recv, z_send, z_recv, f_send, f_recv, b_send, b_recv, c_send, c_recv, a_send, a_recv, r_send, r_recv, h_send, h_recv,
 ):
     me_s = lax.axis_index("seq")
     me_h = lax.axis_index("head")
@@ -97,10 +97,11 @@
         w_copies[i] = send(
             w_hbm.at[rows, columns_of(k)], wall.at[k, rows], w_send.at[i], w_recv.at[i], me_s, lax.rem(me_h + k, 4))
 
-    send_weights(0, 2, rows_at(core * 128, 64))
-    send_weights(2, 1, eighth)
-    send_weights(3, 3, eighth)
-    send_weights(1, 2, rows_at(core * 128 + 64, 64))
+    direct, shared = 1 + 2 * core, (2, 3 - 2 * core)
+    send_weights(0, direct, rows_at(core * 128, 64))
+    send_weights(2, shared[0], eighth)
+    send_weights(3, shared[1], eighth)
+    send_weights(1, direct, rows_at(core * 128 + 64, 64))
     own.start()
     sibling = partner(0)
     f_copies = {}
@@ -111,18 +112,17 @@
     z_copies = []
 
     def share_weights():
-        for i, k in enumerate((1, 3)):
+        for i, k in enumerate(shared):
             w_copies[2 + i].wait_recv()
             for n in range(3):
                 at = 3 * i + n
                 z_copies.append(send(
                     wall.at[k, eighth], wall.at[k, eighth], z_send.at[at], z_recv.at[at], partner(4 + n), me_h))
 
-    def forward_shared():
-        for i, k in enumerate((1, 3)):
-            for n in range(3):
-                z_copies[3 * i + n].wait_recv()
-            to_sibling(2 + i, k, half)
+    def forward_shared(i):
+        for n in range(3):
+            z_copies[3 * i + n].wait_recv()
+        to_sibling(2 + i, shared[i], half)
 
     row_id = lax.broadcasted_iota(jnp.int32, (BLK, BLK), 0)
     col_id = lax.broadcasted_iota(jnp.int32, (BLK, BLK), 1)
@@ -213,7 +213,7 @@
     right_msgs, left_msgs = {}, {}
 
     def send_right(i, src, dst):
-        right_msgs[i] = send(src, dst, r_send.at[i], r_recv.at[i], me_s, right)
+        right_msgs[i] = send(src, dst, r_send.at[2 + i], r_recv.at[2 + i], me_s, right)
 
     def send_left(i, src, dst):
         left_msgs[i] = send(src, dst, r_send.at[6 + i], r_recv.at[6 + i], me_s, left)
@@ -222,32 +222,33 @@
         rows = slice(u * 512 + j * 256, u * 512 + j * 256 + 256)
         return mm_nt(wall[k], og_ref[rows, :])
 
-    share_weights()
     loads[4].wait()
     started = []
 
-    def first_leg(head, r, to):
+    def straight_leg(head, k, r, to):
         rows = rows_at(head * 128 + r * 64, 64)
         for u in range(2):
-            at = slice(u * 512, u * 512 + 512)
-            p2[head, r, :, at] = mm_nt(wall[2, rows, :], og_ref[at, :]).astype(BF16)
-        i = 6 * head + r
-        started.append(send(p2.at[head, r], r1.at[head, r], r_send.at[i], r_recv.at[i], me_s, to))
-
-    def await_first(head):
+            alone[head, r, u] = mm_nt(wall[k, rows, :], og_ref[u * 512:u * 512 + 512, :]).astype(BF16)
+            i = 4 * head + 2 * r + u
+            started.append(send(alone.at[head, r, u], ra.at[head, r, u], a_send.at[i], a_recv.at[i], me_s, to))
+
+    def await_straight(head, u):
         for r in range(2):
+            i = 4 * head + 2 * r + u
             pltpu.make_async_remote_copy(
-                src_ref=p2.at[head, r], dst_ref=r1.at[head, r], send_sem=r_send.at[6 * head + r],
-                recv_sem=r_recv.at[6 * head + r], device_id=(me_s, left), device_id_type=MESH,
+                src_ref=alone.at[head, r, u], dst_ref=ra.at[head, r, u], send_sem=a_send.at[i], recv_sem=a_recv.at[i],
+                device_id=(me_s, left), device_id_type=MESH,
             ).wait_recv()
 
     for r in range(2):
         w_copies[r].wait_recv()
-        to_sibling(r, 2, rows_at(core * 128 + r * 64, 64))
-        first_leg(core, r, lax.rem(me_h + 1 + 2 * core, 4))
+        to_sibling(r, direct, rows_at(core * 128 + r * 64, 64))
+        straight_leg(core, direct, r, lax.rem(me_h + 3 + 2 * core, 4))
+        if r == 0:
+            share_weights()
     for r in range(2):
         f_copies[r].wait_recv()
-        first_leg(1 - core, r, lax.rem(me_h + 3 - 2 * core, 4))
+        straight_leg(1 - core, 3 - 2 * core, r, lax.rem(me_h + 1 + 2 * core, 4))
 
     def diag_forward(b):
         cols = cols_of(b)
@@ -266,27 +267,28 @@
     pl.loop(0, 4, unroll=4)(diag_forward)
     take_states(1)
     send_states(2)
-    forward_shared()
-
-    def second_leg(head, k, to):
+    forward_shared(0)
+
+    def relay_leg(head, u, to):
         rows = rows_at(head * 128, 128)
-        for u in range(2):
-            alone[head, u] = mm_nt(wall[k, rows, :], og_ref[u * 512:u * 512 + 512, :]).astype(BF16)
-            i = 8 - 6 * head + u
-            started.append(send(
-                alone.at[head, u], rdir.at[head, head, u], r_send.at[i], r_recv.at[i], me_s, to))
-
-    def await_second(head, u):
-        i = 8 - 6 * head + u
+        p2[head, u] = mm_nt(wall[2, rows, :], og_ref[u * 512:u * 512 + 512, :]).astype(BF16)
+        i = 4 * head + u
+        started.append(send(p2.at[head, u], r1.at[head, u], r_send.at[i], r_recv.at[i], me_s, to))
+
+    def await_relay(head, u):
+        i = 4 * head + u
         pltpu.make_async_remote_copy(
-            src_ref=alone.at[head, u], dst_ref=rdir.at[head, head, u], send_sem=r_send.at[i], recv_sem=r_recv.at[i],
+            src_ref=p2.at[head, u], dst_ref=r1.at[head, u], send_sem=r_send.at[i], recv_sem=r_recv.at[i],
             device_id=(me_s, left), device_id_type=MESH,
         ).wait_recv()
 
-    second_leg(core, 1 + 2 * core, lax.rem(me_h + 3 + 2 * core, 4))
-    f_copies[2].wait_recv()
+    for u in range(2):
+        relay_leg(core, u, lax.rem(me_h + 1 + 2 * core, 4))
+        if u == 0:
+            f_copies[2].wait_recv()
+            forward_shared(1)
+        relay_leg(1 - core, u, lax.rem(me_h + 3 - 2 * core, 4))
     f_copies[3].wait_recv()
-    second_leg(1 - core, 3 - 2 * core, lax.rem(me_h + 1 + 2 * core, 4))
     for u in range(2):
         for head, k in ((0, 3), (1, 1)):
             pf[head, u] = mm_nt(wall[k, head * 128:head * 128 + 128, :], og_ref[u * 512:u * 512 + 512, :])
@@ -304,16 +306,13 @@
             part = partial_grad(0, u, j)
             po[0, u, :, at] = part[:128]
             po[1, u, :, at] = part[128:]
-    await_first(0)
-    await_first(1)
     for u in range(2):
-        at = slice(u * 512, u * 512 + 512)
-        for head in range(2):
-            for r in range(2):
-                rows = slice(r * 64, r * 64 + 64)
-                summed[head, u, rows, :] = (pf[head, u, rows, :] + r1[head, r, :, at].astype(F32)).astype(BF16)
-        send_right(4 + u, summed.at[0, u], rdir.at[1, 0, u])
-        send_left(4 + u, summed.at[1, u], rdir.at[0, 1, u])
+        await_relay(0, u)
+        summed[0, u] = (pf[0, u] + r1[0, u].astype(F32)).astype(BF16)
+        send_right(u, summed.at[0, u], rb_sum.at[0, u])
+        await_relay(1, u)
+        summed[1, u] = (pf[1, u] + r1[1, u].astype(F32)).astype(BF16)
+        send_left(u, summed.at[1, u], rb_sum.at[1, u])
     take_states(2)
 
     @pl.loop(0, 8, unroll=4)
@@ -325,28 +324,33 @@
 
     h_copies = {}
 
-    def send_heads(i, slot, piece, to_slot, head):
-        rows = slice(piece * 256, piece * 256 + 256)
+    def send_heads(i, slot, start, size, to_slot, head):
+        rows = slice(start, start + size)
         h_copies[i] = send(hall.at[slot, rows], hall.at[to_slot, rows], h_send.at[i], h_recv.at[i], me_s, head)
 
     for n in range(4):
-        send_heads(n, 0, n, 1, right)
-        send_heads(6 + n, 0, (n + 2) % 4, 3, left)
+        send_heads(n, 0, n * 256, 256, 1, right)
+        send_heads(8 + n, 0, (n + 2) % 4 * 256, 256, 3, left)
 
     def relay_heads(n):
         h_copies[n].wait_recv()
-        send_heads(4 + n, 1, n, 2, right)
-        h_copies[6 + n].wait_recv()
-        send_heads(10 + n, 3, n + 2, 2, left)
+        for half_piece in range(2):
+            send_heads(4 + 2 * n + half_piece, 1, n * 256 + half_piece * 128, 128, 2, right)
+        h_copies[8 + n].wait_recv()
+        for half_piece in range(2):
+            send_heads(12 + 2 * n + half_piece, 3, 512 + n * 256 + half_piece * 128, 128, 2, left)
 
     def take_head_grad(u):
         at = slice(u * 512, u * 512 + 512)
-        await_second(0, u)
-        await_second(1, u)
-        right_msgs[4 + u].wait_recv()
-        left_msgs[4 + u].wait_recv()
-        for h in range(2):
-            gt[h, :, at] = (po[h, u] + rdir[0, h, u].astype(F32) + rdir[1, h, u].astype(F32)).astype(BF16)
+        await_straight(0, u)
+        await_straight(1, u)
+        right_msgs[u].wait_recv()
+        left_msgs[u].wait_recv()
+        for h in range(2):
+            for r in range(2):
+                rows = slice(r * 64, r * 64 + 64)
+                gt[h, rows, at] = (
+                    po[h, u, rows, :] + ra[h, r, u].astype(F32) + rb_sum[h, u, rows, :].astype(F32)).astype(BF16)
         for h in range(2):
             grads = mm_nt(wq[h, 3:, :, at].reshape(DEV_BITS * 128, 512), gt[h, :, at])
             for step in range(DEV_BITS):
@@ -459,7 +463,7 @@
     send_grads(0)
     for n in (2, 3):
         h_copies[n].wait_recv()
-        h_copies[6 + n].wait_recv()
+        h_copies[8 + n].wait_recv()
 
     @pl.loop(0, 4, unroll=2)
     def _(b):
@@ -486,10 +490,10 @@
     store(dk_ref, dk_out)
     store(dv_ref, dv_out)
 
-    for n in range(2):
-        for i, b in ((4 + n, n), (10 + n, n + 2)):
+    for n in range(4):
+        for i, b in ((4 + n, n), (12 + n, n + 4)):
             h_copies[i].wait_recv()
-            rows = slice(b * 256, b * 256 + 256)
+            rows = slice(b * 128, b * 128 + 128)
             lo_ref[rows, :] = (acc[rows, :] + mm(hall[2, rows, :], wall[2])).astype(BF16)
             store(lo_ref.at[rows], lo_out.at[rows])
 
@@ -561,22 +565,23 @@
             vmem((2, DEV_BITS, 128, 128), F32),
             vmem((2, 128, 128), F32),
             vmem((2, 7, 128, 128), F32),
-            vmem((2, 2, 64, 1024), BF16),
             vmem((2, 2, 128, 512), BF16),
+            vmem((2, 2, 2, 64, 512), BF16),
             vmem((2, 2, 128, 512), F32),
             vmem((2, 2, 128, 512), F32),
             vmem((2, 2, 128, 512), BF16),
-            vmem((2, 2, 64, 1024), BF16),
-            vmem((2, 2, 2, 128, 512), BF16),
+            vmem((2, 2, 128, 512), BF16),
+            vmem((2, 2, 2, 64, 512), BF16),
+            vmem((2, 2, 128, 512), BF16),
             vmem((4, 1024, 256), BF16),
             vmem((2, 128, 1024), F32),
             vmem((2, 128, 1024), F32),
             vmem((2, 128, 1024), F32),
             vmem((1024, 512), F32),
-            dma((5,)), dma((8,)), dma,
+            dma((5,)), dma((12,)), dma,
             dma((4,)), dma((4,)), dma((6,)), dma((6,)), dma((4,)), dma((4,)),
             dma((7,)), dma((7,)), dma((7,)), dma((7,)),
-            dma((12,)), dma((12,)), dma((12,)), dma((12,)),
+            dma((8,)), dma((8,)), dma((8,)), dma((8,)), dma((16,)), dma((16,)),
         ],
         compiler_params=pltpu.CompilerParams(
             collective_id=0, has_side_effects=True, vmem_limit_bytes=40 * 1024 * 1024),

time: 52.1 us -> 53.7 us (1.031); the launches traced: 51.5 us -> 53.6 us
  Pallas kernels: 50.8 us -> 53 us
    pallas_call x1, Pallas kernels: 49.3 us -> 51.4 us  [per_device(): pl.pallas_call(kernel, out_shape=shapes, in_specs=[hbm] * 6, out_specs=[a...]
where the time goes in v4:
time: 53.7 us; the launch traced here: 53.6 us
  Pallas kernels  53 us (99%)
  between operations  0.64 us (1%)
    pallas_call x1, Pallas kernels, per_device(): pl.pallas_call(kernel, out_shape=shapes, in_specs=[hbm] * 6, out_specs=[a...  51.4 us
    pallas_call x1, Pallas kernels, per_device(): pl.pallas_call(copy_kernel, out_shape=shapes, in_specs=[anywhere] * 5, ou...  1.56 us

profile of v4, /device:TPU:1, one launch (start us, length us, event | category | flops | bytes accessed | tf_op | source)
XLA Modules:
  0.0 53.6 jit_solution(4513473180385031311)
XLA Ops:
  0.6 51.4 %shard_map.101 = (bf16[1024,512]{1,0:T(8,128)(2,1)S(1)}, bf16[1024,2,128]{2,1,0:T(2,128)(2,1)S(1)}, bf16[1024,2,128]{2,1,0:T(2,128)(2,1)S(1)}, bf16[1024,2,128]{2,1,0:T(2,128)(2,1)S(1)}, f32[16,2,1024]{2,1,0:T(2,128)S(1)}) custom-call(bf16[1024,2,128]{2,1,0:T(2,128)(2,1)} %q_in.1, bf16[1024,2,128]{2,1,0:T(2,128)(2,1)} %k_in.1, bf16[1024,2,128]{2,1,0:T(2,128)(2,1)} %v_in.1, ...), custom_call_target="tpu_custom_call" | custom-call | flops 6000000000 | bytes 8388608 | tf_op jit(solution)/shard_map/pallas_call | solution.py:532
  52.1 1.6 %shard_map.102 = (bf16[1024,512]{1,0:T(8,128)(2,1)}, bf16[1024,2,128]{2,1,0:T(2,128)(2,1)}, bf16[1024,2,128]{2,1,0:T(2,128)(2,1)}, bf16[1024,2,128]{2,1,0:T(2,128)(2,1)}, f32[16,2,1024]{2,1,0:T(2,128)}) custom-call(bf16[1024,512]{1,0:T(8,128)(2,1)S(1)} %get-tuple-element.10.refs_0_, bf16[1024,2,128]{2,1,0:T(2,128)(2,1)S(1)} %get-tuple-element.11.refs_1_, ...), custom_call_target="tpu_custom_call" | custom-call | bytes 6291456 | tf_op jit(solution)/shard_map/pallas_call | solution.py:593

commit v5 on v3

--- a/solution.py
+++ b/solution.py
@@ -38,7 +38,7 @@
     lo_out, dq_out, dk_out, dv_out, wg_out,
     q_ref, k_ref, v_ref, lw_ref, og_ref, lo_ref, dq_ref, dk_ref, dv_ref, wg_ref, kn, vn,
     wall, wsc, lev_ref, qt, kt, vt, gt, wq, st_ref, mix_ref, near, tb, tl, tlt, ot,
-    sb, rb, cb, rcb, tst, tstt, lg, xf, llg,
+    sb, rb, cb, rcb, cs, cr, dkn, dvn, tst, tstt, lg, xf, llg,
     p2, alone, pf, po, summed, r1, rdir, hall, dqa, dka, dva, acc,
     in_sem, out_sem, own_sem, w_send, w_recv, z_send, z_recv, f_send, f_recv, b_send, b_recv, c_send, c_recv, r_send, r_recv, h_send, h_recv,
 ):
@@ -353,31 +353,65 @@
                 piece = grads[step * 128:step * 128 + 128]
                 lg[h, step] = piece if u == 0 else lg[h, step] + piece
 
-    for h in range(2):
-        xf[h] = jnp.zeros((128, 128), F32)
-
     c_copies = {}
 
-    def send_grads(phase):
-        for h in range(2):
-            if phase == 0:
-                cb[0, h] = (xf[h] + lg[h, 0] * bit_of(0).astype(F32)).astype(BF16)
-            else:
-                for i in range(2):
-                    slot = 2 * phase - 1 + i
-                    cb[slot, h] = (xf[h] + lg[h, slot] * bit_of(slot).astype(F32)).astype(BF16)
+    def swap_shares():
+        other = 1 - core
+        for n, slot in enumerate((3, 4, 1, 2)):
+            cs[n] = lg[other, slot].astype(BF16)
+        for h in range(2):
+            cs[4 + h] = lg[h, 0].astype(BF16)
+        for n, (start, size) in enumerate(((0, 2), (2, 4))):
+            at = slice(start, start + size)
+            c_copies[7 + n] = send(cs.at[at], cr.at[at], c_send.at[7 + n], c_recv.at[7 + n], sibling, me_h)
+
+    def share_of(slot, n):
+        return (lg[core, slot] + cr[n].astype(F32)) * bit_of(slot).astype(F32)
+
+    def pass_on(phase):
         for n, step in enumerate(PHASES[phase]):
-            slot = 2 * phase - 1 + min(n, 1) if phase else 0
-            c_copies[step] = send(cb.at[slot], rcb.at[step], c_send.at[step], c_recv.at[step], partner(step), me_h)
-
-    def take_grads(phase):
+            c_copies[step] = send(
+                cb.at[2 * phase - 2 + min(n, 1)], rcb.at[step], c_send.at[step], c_recv.at[step], partner(step), me_h)
+
+    def await_steps(phase):
+        got = None
         for step in PHASES[phase]:
             c_copies[step].wait_recv()
-        for h in range(2):
-            total_grad = xf[h]
-            for step in PHASES[phase]:
-                total_grad = total_grad + rcb[step, h].astype(F32)
-            xf[h] = total_grad
+            piece = rcb[step].astype(F32)
+            got = piece if got is None else got + piece
+        return got
+
+    def grads_to_z():
+        c_copies[7].wait_recv()
+        cb[2] = share_of(3, 0).astype(BF16)
+        cb[3] = share_of(4, 1).astype(BF16)
+        pass_on(2)
+
+    def grads_to_y():
+        c_copies[8].wait_recv()
+        got = await_steps(2)
+        xf[0] = got
+        cb[0] = (got + share_of(1, 2)).astype(BF16)
+        cb[1] = (got + share_of(2, 3)).astype(BF16)
+        pass_on(1)
+
+    def swap_results():
+        got = xf[0] + await_steps(1)
+        xf[0] = got
+        cb[4] = got.astype(BF16)
+        c_copies[0] = send(cb.at[4], rcb.at[0], c_send.at[0], c_recv.at[0], sibling, me_h)
+
+    def final_grads():
+        c_copies[0].wait_recv()
+        mine = xf[0]
+        theirs = rcb[0].astype(F32)
+        second = core.astype(F32)
+        first = 1.0 - second
+        near_share = (1 - bit_of(0)).astype(F32)
+        return [
+            mine * first + theirs * second + cr[4].astype(F32) * near_share,
+            mine * second + theirs * first + cr[5].astype(F32) * near_share,
+        ]
 
     def diag_backward(b):
         cols = cols_of(b)
@@ -423,16 +457,16 @@
     take_head_grad(0)
     pl.loop(0, 4, unroll=4)(diag_backward)
     take_head_grad(1)
-    send_grads(2)
+    swap_shares()
     pl.loop(0, 4, unroll=4)(far_backward)
+    grads_to_z()
     pl.loop(4, 8, unroll=4)(diag_backward)
     relay_heads(0)
     relay_heads(1)
-    take_grads(2)
-    send_grads(1)
-    pl.loop(4, 8, unroll=4)(far_backward)
     for h in range(2):
         local_backward(h)
+    grads_to_y()
+    pl.loop(4, 8, unroll=4)(far_backward)
 
     stores = []
 
@@ -455,8 +489,19 @@
         rows = pl.ds(pl.multiple_of(b * 256, 256), 256)
         acc[rows, :] = mm(hall[0, rows, :], wall[0])
 
-    take_grads(1)
-    send_grads(0)
+    for b in range(8):
+        at = slice(b * BLK, b * BLK + BLK)
+        for h in range(2):
+            dk, dv = dka[h, :, at], dva[h, :, at]
+            parts = [llg[h, slot] for slot, (c, first, size) in enumerate(LOCAL_PAIRS) if first - size <= b < first]
+            if parts:
+                x = functools.reduce(lambda a, p: a + p, parts)
+                dk = dk + mm(x.astype(BF16), vt[h, :, at])
+                dv = dv + mm(x.T.astype(BF16), kt[h, :, at])
+            dkn[h, at, :] = dk.T
+            dvn[h, at, :] = dv.T
+
+    swap_results()
     for n in (2, 3):
         h_copies[n].wait_recv()
         h_copies[6 + n].wait_recv()
@@ -466,22 +511,13 @@
         rows = pl.ds(pl.multiple_of(b * 256, 256), 256)
         acc[rows, :] = acc[rows, :] + mm(hall[1, rows, :], wall[1]) + mm(hall[3, rows, :], wall[3])
 
-    take_grads(0)
-
-    for b in range(8):
-        at = slice(b * BLK, b * BLK + BLK)
-        dks, dvs = [], []
-        for h in range(2):
-            x = xf[h]
-            for slot, (c, first, size) in enumerate(LOCAL_PAIRS):
-                if first - size <= b < first:
-                    x = x + llg[h, slot]
-            dk = dka[h, :, at] + mm(x.astype(BF16), vt[h, :, at])
-            dv = dva[h, :, at] + mm(x.T.astype(BF16), kt[h, :, at])
-            dks.append(dk.T.astype(BF16))
-            dvs.append(dv.T.astype(BF16))
-        dk_ref[at] = jnp.concatenate(dks, axis=1).reshape(BLK, 2, 128)
-        dv_ref[at] = jnp.concatenate(dvs, axis=1).reshape(BLK, 2, 128)
+    late = [x.astype(BF16) for x in final_grads()]
+    for b in range(4):
+        at = slice(b * 256, b * 256 + 256)
+        dk = [(dkn[h, at, :] + mm_nt(vn[h, at, :], late[h])).astype(BF16) for h in range(2)]
+        dv = [(dvn[h, at, :] + mm(kn[h, at, :], late[h])).astype(BF16) for h in range(2)]
+        dk_ref[at] = jnp.concatenate(dk, axis=1).reshape(256, 2, 128)
+        dv_ref[at] = jnp.concatenate(dv, axis=1).reshape(256, 2, 128)
 
     store(dk_ref, dk_out)
     store(dv_ref, dv_out)
@@ -554,8 +590,12 @@
             vmem((2, 128, 1024), F32),
             vmem((3, 2, 128, 128), BF16),
             vmem((7, 2, 128, 128), BF16),
-            vmem((5, 2, 128, 128), BF16),
-            vmem((7, 2, 128, 128), BF16),
+            vmem((5, 128, 128), BF16),
+            vmem((7, 128, 128), BF16),
+            vmem((6, 128, 128), BF16),
+            vmem((6, 128, 128), BF16),
+            vmem((2, 1024, 128), F32),
+            vmem((2, 1024, 128), F32),
             vmem((2, DEV_BITS * 128, 128), BF16),
             vmem((2, 128, DEV_BITS * 128), BF16),
             vmem((2, DEV_BITS, 128, 128), F32),
@@ -575,7 +615,7 @@
             vmem((1024, 512), F32),
             dma((5,)), dma((8,)), dma,
             dma((4,)), dma((4,)), dma((6,)), dma((6,)), dma((4,)), dma((4,)),
-            dma((7,)), dma((7,)), dma((7,)), dma((7,)),
+            dma((7,)), dma((7,)), dma((9,)), dma((9,)),
             dma((12,)), dma((12,)), dma((12,)), dma((12,)),
         ],
         compiler_params=pltpu.CompilerParams(

time: 52.1 us -> 52.3 us (level)
  no operation moved by 1% of the time
where the time goes in v5:
time: 52.3 us; the launch traced here: 51.6 us
  Pallas kernels  50.8 us (97%)
  between operations  0.8 us (2%)
    pallas_call x1, Pallas kernels, per_device(): pl.pallas_call(kernel, out_shape=shapes, in_specs=[hbm] * 6, out_specs=[a...  49.3 us
    pallas_call x1, Pallas kernels, per_device(): pl.pallas_call(copy_kernel, out_shape=shapes, in_specs=[anywhere] * 5, ou...  1.56 us

profile of v5, /device:TPU:1, one launch (start us, length us, event | category | flops | bytes accessed | tf_op | source)
XLA Modules:
  0.0 51.6 jit_solution(6431196394860101403)
XLA Ops:
  0.6 49.3 %shard_map.101 = (bf16[1024,512]{1,0:T(8,128)(2,1)S(1)}, bf16[1024,2,128]{2,1,0:T(2,128)(2,1)S(1)}, bf16[1024,2,128]{2,1,0:T(2,128)(2,1)S(1)}, bf16[1024,2,128]{2,1,0:T(2,128)(2,1)S(1)}, f32[16,2,1024]{2,1,0:T(2,128)S(1)}) custom-call(bf16[1024,2,128]{2,1,0:T(2,128)(2,1)} %q_in.1, bf16[1024,2,128]{2,1,0:T(2,128)(2,1)} %k_in.1, bf16[1024,2,128]{2,1,0:T(2,128)(2,1)} %v_in.1, ...), custom_call_target="tpu_custom_call" | custom-call | flops 6000000000 | bytes 8388608 | tf_op jit(solution)/shard_map/pallas_call | solution.py:564
  49.9 1.6 %shard_map.102 = (bf16[1024,512]{1,0:T(8,128)(2,1)}, bf16[1024,2,128]{2,1,0:T(2,128)(2,1)}, bf16[1024,2,128]{2,1,0:T(2,128)(2,1)}, bf16[1024,2,128]{2,1,0:T(2,128)(2,1)}, f32[16,2,1024]{2,1,0:T(2,128)}) custom-call(bf16[1024,512]{1,0:T(8,128)(2,1)S(1)} %get-tuple-element.10.refs_0_, bf16[1024,2,128]{2,1,0:T(2,128)(2,1)S(1)} %get-tuple-element.11.refs_1_, ...), custom_call_target="tpu_custom_call" | custom-call | bytes 6291456 | tf_op jit(solution)/shard_map/pallas_call | solution.py:628

commit v6 on v5

--- a/solution.py
+++ b/solution.py
@@ -39,8 +39,8 @@
     q_ref, k_ref, v_ref, lw_ref, og_ref, lo_ref, dq_ref, dk_ref, dv_ref, wg_ref, kn, vn,
     wall, wsc, lev_ref, qt, kt, vt, gt, wq, st_ref, mix_ref, near, tb, tl, tlt, ot,
     sb, rb, cb, rcb, cs, cr, dkn, dvn, tst, tstt, lg, xf, llg,
-    p2, alone, pf, po, summed, r1, rdir, hall, dqa, dka, dva, acc,
-    in_sem, out_sem, own_sem, w_send, w_recv, z_send, z_recv, f_send, f_recv, b_send, b_recv, c_send, c_recv, r_send, r_recv, h_send, h_recv,
+    p2, alone, pf, po, summed, r1, ra, rb_sum, hall, dqa, dka, dva, acc,
+    in_sem, out_sem, own_sem, w_send, w_recv, z_send, z_recv, f_send, f_recv, b_send, b_recv, c_send, c_recv, a_send, a_recv, r_send, r_recv, h_send, h_recv,
 ):
     me_s = lax.axis_index("seq")
     me_h = lax.axis_index("head")
@@ -97,10 +97,11 @@
         w_copies[i] = send(
             w_hbm.at[rows, columns_of(k)], wall.at[k, rows], w_send.at[i], w_recv.at[i], me_s, lax.rem(me_h + k, 4))
 
-    send_weights(0, 2, rows_at(core * 128, 64))
-    send_weights(2, 1, eighth)
-    send_weights(3, 3, eighth)
-    send_weights(1, 2, rows_at(core * 128 + 64, 64))
+    direct, shared = 1 + 2 * core, (2, 3 - 2 * core)
+    send_weights(0, direct, rows_at(core * 128, 64))
+    send_weights(2, shared[0], eighth)
+    send_weights(3, shared[1], eighth)
+    send_weights(1, direct, rows_at(core * 128 + 64, 64))
     own.start()
     sibling = partner(0)
     f_copies = {}
@@ -111,18 +112,17 @@
     z_copies = []
 
     def share_weights():
-        for i, k in enumerate((1, 3)):
+        for i, k in enumerate(shared):
             w_copies[2 + i].wait_recv()
             for n in range(3):
                 at = 3 * i + n
                 z_copies.append(send(
                     wall.at[k, eighth], wall.at[k, eighth], z_send.at[at], z_recv.at[at], partner(4 + n), me_h))
 
-    def forward_shared():
-        for i, k in enumerate((1, 3)):
-            for n in range(3):
-                z_copies[3 * i + n].wait_recv()
-            to_sibling(2 + i, k, half)
+    def forward_shared(i):
+        for n in range(3):
+            z_copies[3 * i + n].wait_recv()
+        to_sibling(2 + i, shared[i], half)
 
     row_id = lax.broadcasted_iota(jnp.int32, (BLK, BLK), 0)
     col_id = lax.broadcasted_iota(jnp.int32, (BLK, BLK), 1)
@@ -189,15 +189,54 @@
                 xf[h] = xf[h] + got[0] + far
 
     send_states(0)
+    right_msgs, left_msgs = {}, {}
+
+    def send_right(i, src, dst):
+        right_msgs[i] = send(src, dst, r_send.at[2 + i], r_recv.at[2 + i], me_s, right)
+
+    def send_left(i, src, dst):
+        left_msgs[i] = send(src, dst, r_send.at[6 + i], r_recv.at[6 + i], me_s, left)
+
+    def partial_grad(k, u, j):
+        rows = slice(u * 512 + j * 256, u * 512 + j * 256 + 256)
+        return mm_nt(wall[k], og_ref[rows, :])
+
+    loads[4].wait()
+    started = []
+
+    def straight_leg(head, k, r, to):
+        rows = rows_at(head * 128 + r * 64, 64)
+        for u in range(2):
+            alone[head, r, u] = mm_nt(wall[k, rows, :], og_ref[u * 512:u * 512 + 512, :]).astype(BF16)
+            i = 4 * head + 2 * r + u
+            started.append(send(alone.at[head, r, u], ra.at[head, r, u], a_send.at[i], a_recv.at[i], me_s, to))
+
+    def await_straight(head, u):
+        for r in range(2):
+            i = 4 * head + 2 * r + u
+            pltpu.make_async_remote_copy(
+                src_ref=alone.at[head, r, u], dst_ref=ra.at[head, r, u], send_sem=a_send.at[i], recv_sem=a_recv.at[i],
+                device_id=(me_s, left), device_id_type=MESH,
+            ).wait_recv()
+
+    for r in range(2):
+        w_copies[r].wait_recv()
+        to_sibling(r, direct, rows_at(core * 128 + r * 64, 64))
+        straight_leg(core, direct, r, lax.rem(me_h + 3 + 2 * core, 4))
+        if r == 0:
+            share_weights()
+    take_states(0)
+    send_states(1)
+    for r in range(2):
+        f_copies[r].wait_recv()
+        straight_leg(1 - core, 3 - 2 * core, r, lax.rem(me_h + 1 + 2 * core, 4))
+
     loads[2].wait()
     loads[3].wait()
 
     for h in range(2):
         for l in range(LOCAL_LEVELS + DEV_BITS):
             wsc[h, l:l + 1, :] = lw_ref[l, h:h + 1, :] * scale_of(l)
-
-    take_states(0)
-    send_states(1)
 
     @pl.loop(0, 8, unroll=4)
     def _(b):
@@ -209,45 +248,6 @@
             qf = qb.astype(F32)
             for c in range(3 + DEV_BITS):
                 wq[h, c, :, cols] = (qf * wsc[h, DIAG_LEVELS + c:DIAG_LEVELS + c + 1, cols]).astype(BF16)
-
-    right_msgs, left_msgs = {}, {}
-
-    def send_right(i, src, dst):
-        right_msgs[i] = send(src, dst, r_send.at[i], r_recv.at[i], me_s, right)
-
-    def send_left(i, src, dst):
-        left_msgs[i] = send(src, dst, r_send.at[6 + i], r_recv.at[6 + i], me_s, left)
-
-    def partial_grad(k, u, j):
-        rows = slice(u * 512 + j * 256, u * 512 + j * 256 + 256)
-        return mm_nt(wall[k], og_ref[rows, :])
-
-    share_weights()
-    loads[4].wait()
-    started = []
-
-    def first_leg(head, r, to):
-        rows = rows_at(head * 128 + r * 64, 64)
-        for u in range(2):
-            at = slice(u * 512, u * 512 + 512)
-            p2[head, r, :, at] = mm_nt(wall[2, rows, :], og_ref[at, :]).astype(BF16)
-        i = 6 * head + r
-        started.append(send(p2.at[head, r], r1.at[head, r], r_send.at[i], r_recv.at[i], me_s, to))
-
-    def await_first(head):
-        for r in range(2):
-            pltpu.make_async_remote_copy(
-                src_ref=p2.at[head, r], dst_ref=r1.at[head, r], send_sem=r_send.at[6 * head + r],
-                recv_sem=r_recv.at[6 * head + r], device_id=(me_s, left), device_id_type=MESH,
-            ).wait_recv()
-
-    for r in range(2):
-        w_copies[r].wait_recv()
-        to_sibling(r, 2, rows_at(core * 128 + r * 64, 64))
-        first_leg(core, r, lax.rem(me_h + 1 + 2 * core, 4))
-    for r in range(2):
-        f_copies[r].wait_recv()
-        first_leg(1 - core, r, lax.rem(me_h + 3 - 2 * core, 4))
 
     def diag_forward(b):
         cols = cols_of(b)
@@ -264,29 +264,31 @@
             ot[h, :, cols] = mm(vt[h, :, cols], weighted)
 
     pl.loop(0, 4, unroll=4)(diag_forward)
-    take_states(1)
-    send_states(2)
-    forward_shared()
-
-    def second_leg(head, k, to):
+    forward_shared(0)
+
+    def relay_leg(head, u, to):
         rows = rows_at(head * 128, 128)
-        for u in range(2):
-            alone[head, u] = mm_nt(wall[k, rows, :], og_ref[u * 512:u * 512 + 512, :]).astype(BF16)
-            i = 8 - 6 * head + u
-            started.append(send(
-                alone.at[head, u], rdir.at[head, head, u], r_send.at[i], r_recv.at[i], me_s, to))
-
-    def await_second(head, u):
-        i = 8 - 6 * head + u
+        p2[head, u] = mm_nt(wall[2, rows, :], og_ref[u * 512:u * 512 + 512, :]).astype(BF16)
+        i = 4 * head + u
+        started.append(send(p2.at[head, u], r1.at[head, u], r_send.at[i], r_recv.at[i], me_s, to))
+
+    def await_relay(head, u):
+        i = 4 * head + u
         pltpu.make_async_remote_copy(
-            src_ref=alone.at[head, u], dst_ref=rdir.at[head, head, u], send_sem=r_send.at[i], recv_sem=r_recv.at[i],
+            src_ref=p2.at[head, u], dst_ref=r1.at[head, u], send_sem=r_send.at[i], recv_sem=r_recv.at[i],
             device_id=(me_s, left), device_id_type=MESH,
         ).wait_recv()
 
-    second_leg(core, 1 + 2 * core, lax.rem(me_h + 3 + 2 * core, 4))
-    f_copies[2].wait_recv()
+    for u in range(2):
+        relay_leg(core, u, lax.rem(me_h + 1 + 2 * core, 4))
+        if u == 0:
+            f_copies[2].wait_recv()
+            forward_shared(1)
+        relay_leg(1 - core, u, lax.rem(me_h + 3 - 2 * core, 4))
+        if u == 0:
+            take_states(1)
+            send_states(2)
     f_copies[3].wait_recv()
-    second_leg(1 - core, 3 - 2 * core, lax.rem(me_h + 1 + 2 * core, 4))
     for u in range(2):
         for head, k in ((0, 3), (1, 1)):
             pf[head, u] = mm_nt(wall[k, head * 128:head * 128 + 128, :], og_ref[u * 512:u * 512 + 512, :])
@@ -304,16 +306,13 @@
             part = partial_grad(0, u, j)
             po[0, u, :, at] = part[:128]
             po[1, u, :, at] = part[128:]
-    await_first(0)
-    await_first(1)
     for u in range(2):
-        at = slice(u * 512, u * 512 + 512)
-        for head in range(2):
-            for r in range(2):
-                rows = slice(r * 64, r * 64 + 64)
-                summed[head, u, rows, :] = (pf[head, u, rows, :] + r1[head, r, :, at].astype(F32)).astype(BF16)
-        send_right(4 + u, summed.at[0, u], rdir.at[1, 0, u])
-        send_left(4 + u, summed.at[1, u], rdir.at[0, 1, u])
+        await_relay(0, u)
+        summed[0, u] = (pf[0, u] + r1[0, u].astype(F32)).astype(BF16)
+        send_right(u, summed.at[0, u], rb_sum.at[0, u])
+        await_relay(1, u)
+        summed[1, u] = (pf[1, u] + r1[1, u].astype(F32)).astype(BF16)
+        send_left(u, summed.at[1, u], rb_sum.at[1, u])
     take_states(2)
 
     @pl.loop(0, 8, unroll=4)
@@ -341,12 +340,15 @@
 
     def take_head_grad(u):
         at = slice(u * 512, u * 512 + 512)
-        await_second(0, u)
-        await_second(1, u)
-        right_msgs[4 + u].wait_recv()
-        left_msgs[4 + u].wait_recv()
-        for h in range(2):
-            gt[h, :, at] = (po[h, u] + rdir[0, h, u].astype(F32) + rdir[1, h, u].astype(F32)).astype(BF16)
+        await_straight(0, u)
+        await_straight(1, u)
+        right_msgs[u].wait_recv()
+        left_msgs[u].wait_recv()
+        for h in range(2):
+            for r in range(2):
+                rows = slice(r * 64, r * 64 + 64)
+                gt[h, rows, at] = (
+                    po[h, u, rows, :] + ra[h, r, u].astype(F32) + rb_sum[h, u, rows, :].astype(F32)).astype(BF16)
         for h in range(2):
             grads = mm_nt(wq[h, 3:, :, at].reshape(DEV_BITS * 128, 512), gt[h, :, at])
             for step in range(DEV_BITS):
@@ -601,13 +603,14 @@
             vmem((2, DEV_BITS, 128, 128), F32),
             vmem((2, 128, 128), F32),
             vmem((2, 7, 128, 128), F32),
-            vmem((2, 2, 64, 1024), BF16),
             vmem((2, 2, 128, 512), BF16),
+            vmem((2, 2, 2, 64, 512), BF16),
             vmem((2, 2, 128, 512), F32),
             vmem((2, 2, 128, 512), F32),
             vmem((2, 2, 128, 512), BF16),
-            vmem((2, 2, 64, 1024), BF16),
-            vmem((2, 2, 2, 128, 512), BF16),
+            vmem((2, 2, 128, 512), BF16),
+            vmem((2, 2, 2, 64, 512), BF16),
+            vmem((2, 2, 128, 512), BF16),
             vmem((4, 1024, 256), BF16),
             vmem((2, 128, 1024), F32),
             vmem((2, 128, 1024), F32),
@@ -616,7 +619,7 @@
             dma((5,)), dma((8,)), dma,
             dma((4,)), dma((4,)), dma((6,)), dma((6,)), dma((4,)), dma((4,)),
             dma((7,)), dma((7,)), dma((9,)), dma((9,)),
-            dma((12,)), dma((12,)), dma((12,)), dma((12,)),
+            dma((8,)), dma((8,)), dma((8,)), dma((8,)), dma((12,)), dma((12,)),
         ],
         compiler_params=pltpu.CompilerParams(
             collective_id=0, has_side_effects=True, vmem_limit_bytes=40 * 1024 * 1024),

time: 52.3 us -> 51.3 us (0.981)
  no operation moved by 1% of the time
where the time goes in v6:
time: 51.3 us; the launch traced here: 51.2 us
  Pallas kernels  50.4 us (98%)
  between operations  0.8 us (2%)
    pallas_call x1, Pallas kernels, per_device(): pl.pallas_call(kernel, out_shape=shapes, in_specs=[hbm] * 6, out_specs=[a...  48.8 us
    pallas_call x1, Pallas kernels, per_device(): pl.pallas_call(copy_kernel, out_shape=shapes, in_specs=[anywhere] * 5, ou...  1.56 us

profile of v6, /device:TPU:1, one launch (start us, length us, event | category | flops | bytes accessed | tf_op | source)
XLA Modules:
  0.0 51.2 jit_solution(6498637808488078128)
XLA Ops:
  0.6 48.8 %shard_map.101 = (bf16[1024,512]{1,0:T(8,128)(2,1)S(1)}, bf16[1024,2,128]{2,1,0:T(2,128)(2,1)S(1)}, bf16[1024,2,128]{2,1,0:T(2,128)(2,1)S(1)}, bf16[1024,2,128]{2,1,0:T(2,128)(2,1)S(1)}, f32[16,2,1024]{2,1,0:T(2,128)S(1)}) custom-call(bf16[1024,2,128]{2,1,0:T(2,128)(2,1)} %q_in.1, bf16[1024,2,128]{2,1,0:T(2,128)(2,1)} %k_in.1, bf16[1024,2,128]{2,1,0:T(2,128)(2,1)} %v_in.1, ...), custom_call_target="tpu_custom_call" | custom-call | flops 6000000000 | bytes 8388608 | tf_op jit(solution)/shard_map/pallas_call | solution.py:566
  49.4 1.6 %shard_map.102 = (bf16[1024,512]{1,0:T(8,128)(2,1)}, bf16[1024,2,128]{2,1,0:T(2,128)(2,1)}, bf16[1024,2,128]{2,1,0:T(2,128)(2,1)}, bf16[1024,2,128]{2,1,0:T(2,128)(2,1)}, f32[16,2,1024]{2,1,0:T(2,128)}) custom-call(bf16[1024,512]{1,0:T(8,128)(2,1)S(1)} %get-tuple-element.10.refs_0_, bf16[1024,2,128]{2,1,0:T(2,128)(2,1)S(1)} %get-tuple-element.11.refs_1_, ...), custom_call_target="tpu_custom_call" | custom-call | bytes 6291456 | tf_op jit(solution)/shard_map/pallas_call | solution.py:631

commit v7 on v6

--- a/solution.py
+++ b/solution.py
@@ -294,6 +294,13 @@
             pf[head, u] = mm_nt(wall[k, head * 128:head * 128 + 128, :], og_ref[u * 512:u * 512 + 512, :])
     pl.loop(4, 8, unroll=4)(diag_forward)
 
+    for u in range(2):
+        await_relay(0, u)
+        summed[0, u] = (pf[0, u] + r1[0, u].astype(F32)).astype(BF16)
+        send_right(u, summed.at[0, u], rb_sum.at[0, u])
+        await_relay(1, u)
+        summed[1, u] = (pf[1, u] + r1[1, u].astype(F32)).astype(BF16)
+        send_left(u, summed.at[1, u], rb_sum.at[1, u])
     for h in range(2):
         for slot, (c, first, size) in enumerate(LOCAL_PAIRS):
             at = slice(first * BLK, (first + size) * BLK)
@@ -306,13 +313,6 @@
             part = partial_grad(0, u, j)
             po[0, u, :, at] = part[:128]
             po[1, u, :, at] = part[128:]
-    for u in range(2):
-        await_relay(0, u)
-        summed[0, u] = (pf[0, u] + r1[0, u].astype(F32)).astype(BF16)
-        send_right(u, summed.at[0, u], rb_sum.at[0, u])
-        await_relay(1, u)
-        summed[1, u] = (pf[1, u] + r1[1, u].astype(F32)).astype(BF16)
-        send_left(u, summed.at[1, u], rb_sum.at[1, u])
     take_states(2)
 
     @pl.loop(0, 8, unroll=4)

time: 51.3 us -> 51.1 us (level)
  no operation moved by 1% of the time
where the time goes in v7:
time: 51.1 us; the launch traced here: 51 us
  Pallas kernels  50.2 us (98%)
  between operations  0.8 us (2%)
    pallas_call x1, Pallas kernels, per_device(): pl.pallas_call(kernel, out_shape=shapes, in_specs=[hbm] * 6, out_specs=[a...  48.6 us
    pallas_call x1, Pallas kernels, per_device(): pl.pallas_call(copy_kernel, out_shape=shapes, in_specs=[anywhere] * 5, ou...  1.56 us

profile of v7, /device:TPU:1, one launch (start us, length us, event | category | flops | bytes accessed | tf_op | source)
XLA Modules:
  0.0 51.0 jit_solution(7817469265155507630)
XLA Ops:
  0.6 48.6 %shard_map.101 = (bf16[1024,512]{1,0:T(8,128)(2,1)S(1)}, bf16[1024,2,128]{2,1,0:T(2,128)(2,1)S(1)}, bf16[1024,2,128]{2,1,0:T(2,128)(2,1)S(1)}, bf16[1024,2,128]{2,1,0:T(2,128)(2,1)S(1)}, f32[16,2,1024]{2,1,0:T(2,128)S(1)}) custom-call(bf16[1024,2,128]{2,1,0:T(2,128)(2,1)} %q_in.1, bf16[1024,2,128]{2,1,0:T(2,128)(2,1)} %k_in.1, bf16[1024,2,128]{2,1,0:T(2,128)(2,1)} %v_in.1, ...), custom_call_target="tpu_custom_call" | custom-call | flops 6000000000 | bytes 8388608 | tf_op jit(solution)/shard_map/pallas_call | solution.py:566
  49.3 1.6 %shard_map.102 = (bf16[1024,512]{1,0:T(8,128)(2,1)}, bf16[1024,2,128]{2,1,0:T(2,128)(2,1)}, bf16[1024,2,128]{2,1,0:T(2,128)(2,1)}, bf16[1024,2,128]{2,1,0:T(2,128)(2,1)}, f32[16,2,1024]{2,1,0:T(2,128)}) custom-call(bf16[1024,512]{1,0:T(8,128)(2,1)S(1)} %get-tuple-element.10.refs_0_, bf16[1024,2,128]{2,1,0:T(2,128)(2,1)S(1)} %get-tuple-element.11.refs_1_, ...), custom_call_target="tpu_custom_call" | custom-call | bytes 6291456 | tf_op jit(solution)/shard_map/pallas_call | solution.py:631
